TPU v7x, 512 devices: a whole 4x8x8 slice. The times are simulated.
512 devices in a mesh: lat: 32 (over z, x), lon: 16 (over y, core).
Axes of the slice: x: 4, y: 8, z: 8, core: 2. Of those that a mesh axis runs over, the one named last changes fastest.
Arguments:
- grid_field: bfloat16 [384, 768, 384], P('lat', 'lon'), may hold values from -6 to 6
- disco_filter: float32 [3, 5, 384], P(None, None, 'lat'), may hold values from -3 to 3
- offsets: int32 [3, 5, 384], P(None, None, 'lat'), may hold values from -2 to 2
- disco_weight: bfloat16 [3, 384, 384], replicated, may hold values from -0.1875 to 0.1875
- legendre: bfloat16 [2, 192, 384, 384], P(None, 'lat', None, 'lon'), as said below
- spec_weight: bfloat16 [2, 384, 384], replicated, may hold values from -0.21875 to 0.21875
- degree_gain: float32 [384, 384], replicated, may hold values from 0.25 to 2.5
Outputs:
- result: bfloat16 [384, 768, 384], P('lat', 'lon')
Inputs may be any that keep to these rules, and one draw needn't show every extreme that they name: legendre[h, p, l, t] is zero wherever the degree l is below the entry's wavenumber (p for h = 0, 383 - p for h = 1).
All inputs are finite; a program needn't handle non-finite values.
Results may differ from a plain program's by a relative error of at most 0.0055.
Values may be sent and summed in bfloat16 or wider, within the bound.
A program may use at most 128 MiB of HBM per device.

v0:
```python
import math

import jax
import jax.numpy as jnp
from jax import lax
from jax.sharding import PartitionSpec as P

NLON = 768
MMAX = 384


def extended(cells, sides, width, closed):
    for axis, dim in sides:
        count = lax.axis_size(axis)
        ends = count if closed else count - 1
        head = lax.slice_in_dim(cells, 0, width, axis=dim)
        tail = lax.slice_in_dim(cells, cells.shape[dim] - width, cells.shape[dim], axis=dim)
        cells = jnp.concatenate(
            [
                lax.ppermute(tail, axis, [(i, (i + 1) % count) for i in range(ends)]),
                cells,
                lax.ppermute(head, axis, [((i + 1) % count, i) for i in range(ends)]),
            ],
            axis=dim,
        )
    return cells


def fourier_table(nlon, mmax):
    columns = jnp.arange(2 * mmax, dtype=jnp.int32)
    pair_index = columns // 4
    halves = columns // 2 % 2
    component = columns % 2
    wavenumber = jnp.where(halves == 0, pair_index, mmax - 1 - pair_index)
    longitude = jnp.arange(nlon, dtype=jnp.int32)
    phases = longitude[:, None] * wavenumber[None, :] % nlon
    angles = phases.astype(jnp.float32) * (2.0 * math.pi / nlon)
    norm_scale = 1.0 / math.sqrt(nlon)
    values = jnp.where(component[None, :] == 0, jnp.cos(angles), -jnp.sin(angles)) * norm_scale
    return values.astype(jnp.bfloat16)


def channel_mix(values_in, row_gain, stacked_weight):
    lead_shape = values_in.shape[:-2]
    channels = values_in.shape[-1]
    flattened = values_in.reshape(-1, 2 * channels)
    mixed_rows = jnp.dot(flattened, stacked_weight, preferred_element_type=jnp.float32)
    mixed_rows = mixed_rows.reshape(lead_shape + (2, channels))
    return (mixed_rows * row_gain).astype(jnp.bfloat16)


def on_device(grid_field, disco_filter, offsets, disco_weight, legendre, spec_weight, degree_gain):
    lat_dev, lon_dev, channels = grid_field.shape
    kernel_count = disco_filter.shape[0]
    lon_index = lax.axis_index("lon")
    widened = extended(grid_field, (("lon", 1),), 2, True)
    padded = extended(widened, (("lat", 0),), 2, False)
    wide_cols = padded.shape[1]
    summed = jnp.zeros((kernel_count, lat_dev, lon_dev, channels), jnp.float32)
    for col_step in range(5):
        column_sum = jnp.zeros((kernel_count, lat_dev, wide_cols, channels), jnp.float32)
        for row_step in range(5):
            row_coeff = jnp.where(
                offsets[:, row_step] == col_step - 2, disco_filter[:, row_step], 0.0
            )
            row_block = padded[row_step : row_step + lat_dev].astype(jnp.float32)
            column_sum = column_sum + row_coeff[:, :, None, None] * row_block[None]
        summed = summed + column_sum[:, :, col_step : col_step + lon_dev]
    basis_terms = summed.astype(jnp.bfloat16).reshape(kernel_count, lat_dev * lon_dev, channels)
    disco = jnp.zeros((lat_dev * lon_dev, channels), jnp.float32)
    for basis in range(kernel_count):
        disco = disco + jnp.dot(
            basis_terms[basis], disco_weight[basis], preferred_element_type=jnp.float32
        )
    disco = disco.reshape(lat_dev, lon_dev, channels)
    trig_table = fourier_table(NLON, MMAX)
    full_rows = lax.all_to_all(grid_field, "lon", split_axis=2, concat_axis=1, tiled=True)
    fourier = jnp.einsum(
        "lnc,nk->lkc", full_rows, trig_table, preferred_element_type=jnp.float32
    ).astype(jnp.bfloat16)
    fourier = fourier.reshape(lat_dev, MMAX // 2, 2, 2, -1)
    by_wavenumber = lax.all_to_all(fourier, "lat", split_axis=1, concat_axis=0, tiled=True)
    share = by_wavenumber.shape[4]
    full_table = lax.all_gather(legendre, "lon", axis=3, tiled=True)
    spectrum = jnp.einsum(
        "hilt,tihrc->ihlrc", full_table, by_wavenumber, preferred_element_type=jnp.float32
    )
    spectrum = spectrum.astype(jnp.bfloat16)
    w_real = spec_weight[0]
    w_imag = spec_weight[1]
    stacked_weight = jnp.concatenate(
        [jnp.concatenate([w_real, w_imag], axis=1), jnp.concatenate([-w_imag, w_real], axis=1)],
        axis=0,
    )
    spread = lax.all_to_all(spectrum, "lon", split_axis=2, concat_axis=4, tiled=True)
    local_degrees = spread.shape[2]
    row_gain = lax.dynamic_slice_in_dim(degree_gain, lon_index * local_degrees, local_degrees, 0)
    filtered_part = channel_mix(spread, row_gain[None, None, :, None, :], stacked_weight)
    filtered = lax.all_to_all(filtered_part, "lon", split_axis=4, concat_axis=2, tiled=True)
    returned = jnp.einsum(
        "hilt,ihlrc->tihrc", full_table, filtered, preferred_element_type=jnp.float32
    )
    returned = returned.astype(jnp.bfloat16)
    by_latitude = lax.all_to_all(returned, "lat", split_axis=0, concat_axis=1, tiled=True)
    by_latitude = by_latitude.reshape(lat_dev, 2 * MMAX, share)
    spectral = jnp.einsum(
        "lkc,nk->lnc", by_latitude, trig_table, preferred_element_type=jnp.float32
    ).astype(jnp.bfloat16)
    spectral = lax.all_to_all(spectral, "lon", split_axis=1, concat_axis=2, tiled=True)
    combined = spectral.astype(jnp.float32) + disco
    return (grid_field.astype(jnp.float32) + jax.nn.gelu(combined)).astype(jnp.bfloat16)


def solution(mesh):
    in_specs = (
        P("lat", "lon", None),
        P(None, None, "lat"),
        P(None, None, "lat"),
        P(),
        P(None, "lat", None, "lon"),
        P(),
        P(),
    )
    out_specs = P("lat", "lon", None)
    return jax.shard_map(
        on_device, mesh=mesh, in_specs=in_specs, out_specs=out_specs, check_vma=False
    )
```

profile of v0, /device:TPU:1, one launch (start us, length us, event | category | flops | bytes accessed | tf_op | source)
XLA Modules:
  0.0 310.6 jit_solution(14937966880368758817)
XLA Ops:
  6.5 1.7 copy.59
  9.3 2.7 collective-permute-start
  12.0 4.2 %collective-permute-start.1 = (bf16[12,2,384]{2,1,0:T(2,128)(2,1)S(1)}, bf16[12,2,384]{2,1,0:T(2,128)(2,1)S(1)}, u32[]{:S(2)}, u32[]{:S(2)}) collective-permute-start(bf16[12,2,384]{2,1,0:T(2,128)(2,1)S(1)} %get-tuple-element.46), channel_id=1, source_target_pairs={{1,0},{2,1},{3,2},{4,3},{5,4},{6,5},{7,6},{8,7},{9,8},{10,9},{11,1... | collective-permute-start | bytes 55304 | tf_op jit(solution)/shard_map/ppermute | solution.py:22
  16.2 2.1 copy.53
  18.4 2.6 reshape.463
  21.0 6.9 %all-to-all-start = ((bf16[16,2,6912]{2,1,0:T(2,128)(2,1)}), bf16[16,2,6912]{2,1,0:T(2,128)(2,1)S(1)}, u32[]{:S(2)}, u32[]{:S(2)}) async-start(bf16[16,2,6912]{2,1,0:T(2,128)(2,1)} %reshape.463), calls=%async_computation | async-start | bytes 884736 | tf_op jit(solution)/shard_map/all_to_all | solution.py:77
  31.4 16.1 %all-to-all-done = bf16[16,2,6912]{2,1,0:T(2,128)(2,1)S(1)} async-done(((bf16[16,2,6912]{2,1,0:T(2,128)(2,1)}), bf16[16,2,6912]{2,1,0:T(2,128)(2,1)S(1)}, u32[]{:S(2)}, u32[]{:S(2)}) %all-to-all-start) | async-done | bytes 442400 | tf_op jit(solution)/shard_map/all_to_all | solution.py:77
  47.5 2.0 reshape.464
  50.2 1.3 all_to_all.71
  51.6 10.5 %fusion.28 = f32[768,288]{0,1:S(1)} fusion(bf16[768,288]{0,1:T(8,128)(2,1)S(1)} %bitcast.188, s32[768]{0:T(1024)S(1)} %subtract_select_fusion, pred[768]{0:T(1024)(128)(4,1)S(1)} %fusion.46), kind=kOutput, calls=%fused_computation.27 | convolution fusion | flops 347406336 | bytes 1330944
  62.1 1.1 copy.56
  63.3 3.0 copy.87
  66.3 8.9 %reshape.465 = bf16[32,2,3456]{2,1,0:T(2,128)(2,1)} reshape(bf16[192,12,2,2,24]{4,3,2,1,0:T(2,128)(2,1)} %bitcast.168) | data formatting | bytes 884736
  75.2 11.5 %all-to-all-start.1 = ((bf16[32,2,3456]{2,1,0:T(2,128)(2,1)}), bf16[32,2,3456]{2,1,0:T(2,128)(2,1)S(1)}, u32[]{:S(2)}, u32[]{:S(2)}) async-start(bf16[32,2,3456]{2,1,0:T(2,128)(2,1)} %reshape.465), calls=%async_computation.1 | async-start | bytes 884736 | tf_op jit(solution)/shard_map/all_to_all | solution.py:82
  86.8 1.2 maximum_bitcast_fusion
  88.6 1.5 copy.63
  90.9 3.8 %collective-permute-start.2 = (bf16[2,52,384]{2,1,0:T(8,128)(2,1)}, bf16[2,52,384]{2,1,0:T(8,128)(2,1)}, u32[]{:S(2)}, u32[]{:S(2)}) collective-permute-start(bf16[2,52,384]{2,1,0:T(8,128)(2,1)} %get-tuple-element.39), channel_id=1, source_target_pairs={{0,16},{16,32},{32,48},{48,64},{64,80},{80,96},{96,112},{112,128},... | collective-permute-start | bytes 239624 | tf_op jit(solution)/shard_map/ppermute | solution.py:20
  94.7 1.3 collective-permute-start.3
  96.0 2.2 fusion.69
  98.1 3.9 %all-to-all-done.1 = bf16[32,2,3456]{2,1,0:T(2,128)(2,1)S(1)} async-done(((bf16[32,2,3456]{2,1,0:T(2,128)(2,1)}), bf16[32,2,3456]{2,1,0:T(2,128)(2,1)S(1)}, u32[]{:S(2)}, u32[]{:S(2)}) %all-to-all-start.1) | async-done | bytes 442400 | tf_op jit(solution)/shard_map/all_to_all | solution.py:82
  102.0 4.3 %reshape.466 = bf16[192,12,2,2,24]{4,3,2,1,0:T(2,128)(2,1)} reshape(bf16[32,2,3456]{2,1,0:T(2,128)(2,1)S(1)} %all-to-all-done.1) | data formatting | bytes 884736
  106.3 3.3 %copy.58 = bf16[12,32,6,2,2,24]{5,4,3,2,0,1:T(2,128)(2,1)S(1)} copy(bf16[12,32,6,2,2,24]{5,4,3,0,2,1:T(2,128)(2,1)} %bitcast.169) | data formatting | bytes 884736 | tf_op jit(solution)/shard_map/all_to_all | solution.py:82
  109.6 2.8 fusion.22
  112.5 2.1 copy.61
  114.6 3.8 %reshape.467 = bf16[16,2,6912]{2,1,0:T(2,128)(2,1)} reshape(bf16[384,6,2,2,24]{4,3,2,1,0:T(2,128)(2,1)S(1)} %bitcast.170) | data formatting | bytes 884736
  118.4 6.3 %all-to-all-start.2 = ((bf16[16,2,6912]{2,1,0:T(2,128)(2,1)}), bf16[16,2,6912]{2,1,0:T(2,128)(2,1)S(1)}, u32[]{:S(2)}, u32[]{:S(2)}) async-start(bf16[16,2,6912]{2,1,0:T(2,128)(2,1)} %reshape.467), calls=%async_computation.2 | async-start | bytes 884736 | tf_op jit(solution)/shard_map/all_to_all | solution.py:95
  124.7 1.1 maximum_maximum_fusion
  126.1 2.1 fusion.67
  128.2 11.9 %all-to-all-done.2 = bf16[16,2,6912]{2,1,0:T(2,128)(2,1)S(1)} async-done(((bf16[16,2,6912]{2,1,0:T(2,128)(2,1)}), bf16[16,2,6912]{2,1,0:T(2,128)(2,1)S(1)}, u32[]{:S(2)}, u32[]{:S(2)}) %all-to-all-start.2) | async-done | bytes 442400 | tf_op jit(solution)/shard_map/all_to_all | solution.py:95
  140.1 4.4 %reshape.468 = bf16[384,6,2,2,24]{4,3,2,1,0:T(2,128)(2,1)} reshape(bf16[16,2,6912]{2,1,0:T(2,128)(2,1)S(1)} %all-to-all-done.2) | data formatting | bytes 884736
  144.5 5.8 %copy.86 = bf16[6,2,16,24,2,24]{5,2,4,3,1,0:T(8,128)(2,1)} copy(bf16[6,2,16,24,2,24]{5,4,1,0,3,2:T(2,128)(2,1)} %bitcast.171) | data formatting | bytes 884736 | tf_op jit(solution)/shard_map/all_to_all | solution.py:95
  150.4 4.2 %reshape.458 = bf16[6,2,24,768,1]{3,2,1,0,4:T(8,128)(2,1)S(1)} reshape(bf16[6,2,24,2,16,24]{5,4,3,2,1,0:T(8,128)(2,1)} %bitcast.172) | data formatting | bytes 884736 | tf_op jit(solution)/shard_map/dot_general | solution.py:47
  154.6 2.6 fusion.15
  157.2 6.2 %copy.64 = bf16[6,2,24,2,384]{2,3,1,0,4:T(2,128)(2,1)} copy(bf16[6,2,24,2,384]{4,2,3,1,0:T(8,128)(2,1)} %fusion.15) | data formatting | bytes 884736 | tf_op jit(solution)/shard_map/convert_element_type | solution.py:49
  163.4 8.7 %reshape.469 = bf16[16,2,6912]{2,1,0:T(2,128)(2,1)} reshape(bf16[384,6,2,2,24]{4,3,2,1,0:T(2,128)(2,1)} %bitcast.173) | data formatting | bytes 884736
  172.1 3.9 %all-to-all-start.3 = ((bf16[16,2,6912]{2,1,0:T(2,128)(2,1)}), bf16[16,2,6912]{2,1,0:T(2,128)(2,1)S(1)}, u32[]{:S(2)}, u32[]{:S(2)}) async-start(bf16[16,2,6912]{2,1,0:T(2,128)(2,1)} %reshape.469), calls=%async_computation.3 | async-start | bytes 884736 | tf_op jit(solution)/shard_map/all_to_all | solution.py:99
  176.0 2.1 fusion.68
  178.1 2.1 fusion.70
  180.2 2.1 fusion.71
  182.3 7.4 %all-to-all-done.3 = bf16[16,2,6912]{2,1,0:T(2,128)(2,1)S(1)} async-done(((bf16[16,2,6912]{2,1,0:T(2,128)(2,1)}), bf16[16,2,6912]{2,1,0:T(2,128)(2,1)S(1)}, u32[]{:S(2)}, u32[]{:S(2)}) %all-to-all-start.3) | async-done | bytes 442400 | tf_op jit(solution)/shard_map/all_to_all | solution.py:99
  189.7 4.4 %reshape.470 = bf16[384,6,2,2,24]{4,3,2,1,0:T(2,128)(2,1)} reshape(bf16[16,2,6912]{2,1,0:T(2,128)(2,1)S(1)} %all-to-all-done.3) | data formatting | bytes 884736
  194.1 4.7 %copy.85 = bf16[6,2,24,2,16,24]{2,4,5,3,1,0:T(8,128)(2,1)} copy(bf16[6,2,24,2,16,24]{2,3,1,0,5,4:T(2,128)(2,1)} %bitcast.174) | data formatting | bytes 884736 | tf_op jit(solution)/shard_map/all_to_all | solution.py:99
  198.8 4.5 %all_to_all.82 = bf16[6,2,384,2,24]{2,4,3,1,0:T(8,128)(2,1)} reshape(bf16[6,2,16,24,2,24]{3,2,5,4,1,0:T(8,128)(2,1)} %bitcast.175) | data formatting | bytes 884736 | tf_op jit(solution)/shard_map/all_to_all | solution.py:99
  203.3 3.3 %fusion.19 = bf16[384,6,2,2,24]{0,4,3,2,1:T(8,128)(2,1)} fusion(bf16[6,2,384,2,24]{2,4,3,1,0:T(8,128)(2,1)} %all_to_all.82, bf16[2,6,384,384]{2,3,0,1:T(8,128)(2,1)S(1)} %copy-done.2), kind=kOutput, calls=%fused_computation.23 | convolution fusion | flops 170090496 | bytes 4423680 | tf_op jit(solution)/shard_map/hilt,ihlrc->tihrc/dot_general | solution.py:100
  206.8 5.2 %copy.66 = bf16[384,6,2,2,24]{4,3,2,1,0:T(2,128)(2,1)S(1)} copy(bf16[384,6,2,2,24]{0,4,3,2,1:T(8,128)(2,1)} %fusion.19) | data formatting | bytes 884736 | tf_op jit(solution)/shard_map/convert_element_type | solution.py:103
  212.0 3.8 %reshape.471 = bf16[32,2,3456]{2,1,0:T(2,128)(2,1)} reshape(bf16[384,6,2,2,24]{4,3,2,1,0:T(2,128)(2,1)S(1)} %copy.66) | data formatting | bytes 884736
  215.8 5.6 %all-to-all-start.4 = ((bf16[32,2,3456]{2,1,0:T(2,128)(2,1)}), bf16[32,2,3456]{2,1,0:T(2,128)(2,1)}, u32[]{:S(2)}, u32[]{:S(2)}) async-start(bf16[32,2,3456]{2,1,0:T(2,128)(2,1)} %reshape.471), calls=%async_computation.4 | async-start | bytes 884736 | tf_op jit(solution)/shard_map/all_to_all | solution.py:104
  221.7 11.2 %add_convert_fusion = bf16[3,12,48,384]{3,2,1,0:T(8,128)(2,1)S(1)} fusion(f32[12,48,384]{2,1,0:T(8,128)} %get-tuple-element.32, f32[3,12]{1,0:T(4,128)S(1)} %copy-done.19, f32[12,48,384]{2,1,0:T(8,128)} %get-tuple-element.27, f32[3,12]{1,0:T(4,128)S(1)} %copy-done.39, f32[12,48,384]{2,1,0:T(8,128)} %get-tuple-element.22, f32[3,12]{1,0:T(4,128)S(1)} %copy-done.35, ...), kind=kLoop, calls=%fused_computation.5 | loop fusion | flops 33177600 | bytes 23449104 | tf_op jit(solution)/shard_map/convert_element_type | solution.py:69
  232.9 1.1 fusion.66
  234.0 2.7 all-to-all-done.4
  236.7 8.6 %reshape.472 = bf16[384,6,2,2,24]{4,3,2,1,0:T(2,128)(2,1)S(1)} reshape(bf16[32,2,3456]{2,1,0:T(2,128)(2,1)} %all-to-all-done.4) | data formatting | bytes 884736
  245.3 3.6 %copy.67 = bf16[12,32,6,2,2,24]{5,4,3,2,1,0:T(2,128)(2,1)} copy(bf16[12,32,6,2,2,24]{5,4,3,2,0,1:T(2,128)(2,1)S(1)} %bitcast.176) | data formatting | bytes 884736 | tf_op jit(solution)/shard_map/all_to_all | solution.py:104
  248.8 2.2 copy.68
  251.1 10.1 %fusion.27 = f32[768,288]{0,1:S(1)} fusion(bf16[768,288]{0,1:T(8,128)(2,1)S(1)} %bitcast.189, s32[768]{0:T(1024)S(1)} %copy-done.41, pred[768]{0:T(1024)(128)(4,1)S(1)} %copy-done.43), kind=kOutput, calls=%fused_computation.26 | convolution fusion | flops 347406336 | bytes 1330944
  262.0 3.8 %copy.69 = bf16[12,768,24]{2,0,1:T(8,128)(2,1)S(1)} copy(bf16[12,768,24]{1,2,0:T(8,128)(2,1)} %convert_bitcast_fusion) | data formatting | bytes 884736 | tf_op jit(solution)/shard_map/convert_element_type | solution.py:108
  265.8 4.0 %reshape.473 = bf16[16,2,6912]{2,1,0:T(2,128)(2,1)} reshape(bf16[768,12,24]{2,1,0:T(8,128)(2,1)S(1)} %bitcast.165) | data formatting | bytes 884736
  269.8 6.1 %all-to-all-start.5 = ((bf16[16,2,6912]{2,1,0:T(2,128)(2,1)}), bf16[16,2,6912]{2,1,0:T(2,128)(2,1)}, u32[]{:S(2)}, u32[]{:S(2)}) async-start(bf16[16,2,6912]{2,1,0:T(2,128)(2,1)} %reshape.473), calls=%async_computation.5 | async-start | bytes 884736 | tf_op jit(solution)/shard_map/all_to_all | solution.py:109
  275.9 1.5 fusion.41
  277.9 1.4 convolution_add_fusion
  279.2 12.4 %all-to-all-done.5 = bf16[16,2,6912]{2,1,0:T(2,128)(2,1)} async-done(((bf16[16,2,6912]{2,1,0:T(2,128)(2,1)}), bf16[16,2,6912]{2,1,0:T(2,128)(2,1)}, u32[]{:S(2)}, u32[]{:S(2)}) %all-to-all-start.5) | async-done | bytes 442400 | tf_op jit(solution)/shard_map/all_to_all | solution.py:109
  291.7 4.7 %reshape.474 = bf16[768,12,24]{2,1,0:T(8,128)(2,1)S(1)} reshape(bf16[16,2,6912]{2,1,0:T(2,128)(2,1)} %all-to-all-done.5) | data formatting | bytes 884736
  296.4 3.7 %copy.70 = f32[12,16,48,24]{2,3,1,0:T(8,128)} copy(bf16[12,16,48,24]{3,0,2,1:T(8,128)(2,1)S(1)} %bitcast.166) | data formatting | bytes 1327104 | tf_op jit(solution)/shard_map/convert_element_type | solution.py:110
  300.2 2.1 copy.71
  302.3 1.1 fusion.37
  (111 shorter events, 8.5 us)
Async XLA Ops:
  6.5 81.4 %copy-start = (f32[384,384]{1,0:T(8,128)S(1)}, f32[384,384]{1,0:T(8,128)}, u32[]{:S(2)}) copy-start(f32[384,384]{1,0:T(8,128)} %param.13) | copy-start | bytes 1769476
  6.5 103.1 %all-gather.2.cloned.1.call-start = ((), (), s32[]{:S(2)}) async-start(), calls=%async_computation.6 | async-start | bytes 3760128 | tf_op jit(solution)/shard_map/all_gather | solution.py:84
  8.3 19.6 %copy-start.17 = (f32[3,5,12]{2,0,1:T(4,128)S(1)}, f32[3,5,12]{2,0,1:T(4,128)}, u32[]{:S(2)}) copy-start(f32[3,5,12]{2,0,1:T(4,128)} %param.8) | copy-start | bytes 2164
  8.3 19.6 %copy-start.18 = (s32[3,5,12]{2,0,1:T(4,128)S(1)}, s32[3,5,12]{2,0,1:T(4,128)}, u32[]{:S(2)}) copy-start(s32[3,5,12]{2,0,1:T(4,128)} %param.9) | copy-start | bytes 2164
  8.3 21.5 %copy-start.9 = (bf16[2,384,384]{2,1,0:T(8,128)(2,1)S(1)}, bf16[2,384,384]{2,1,0:T(8,128)(2,1)}, u32[]{:S(2)}) copy-start(bf16[2,384,384]{2,1,0:T(8,128)(2,1)} %param.12) | copy-start | bytes 1769476
  9.3 80.7 %collective-permute-start = (bf16[12,2,384]{2,1,0:T(2,128)(2,1)S(1)}, bf16[12,2,384]{2,1,0:T(2,128)(2,1)S(1)}, u32[]{:S(2)}, u32[]{:S(2)}) collective-permute-start(bf16[12,2,384]{2,1,0:T(2,128)(2,1)S(1)} %get-tuple-element.45), channel_id=1, source_target_pairs={{0,1},{1,2},{2,3},{3,4},{4,5},{5,6},{6,7},{7,8},{8,9},{9,10},{10,1... | collective-permute-start | bytes 55304 | tf_op jit(solution)/shard_map/ppermute | solution.py:20
  12.0 78.0 %collective-permute-start.1 = (bf16[12,2,384]{2,1,0:T(2,128)(2,1)S(1)}, bf16[12,2,384]{2,1,0:T(2,128)(2,1)S(1)}, u32[]{:S(2)}, u32[]{:S(2)}) collective-permute-start(bf16[12,2,384]{2,1,0:T(2,128)(2,1)S(1)} %get-tuple-element.46), channel_id=1, source_target_pairs={{1,0},{2,1},{3,2},{4,3},{5,4},{6,5},{7,6},{8,7},{9,8},{10,9},{11,1... | collective-permute-start | bytes 55304 | tf_op jit(solution)/shard_map/ppermute | solution.py:22
  21.0 26.5 %all-to-all-start = ((bf16[16,2,6912]{2,1,0:T(2,128)(2,1)}), bf16[16,2,6912]{2,1,0:T(2,128)(2,1)S(1)}, u32[]{:S(2)}, u32[]{:S(2)}) async-start(bf16[16,2,6912]{2,1,0:T(2,128)(2,1)} %reshape.463), calls=%async_computation | async-start | bytes 884736 | tf_op jit(solution)/shard_map/all_to_all | solution.py:77
  29.1 22.5 %copy-start.42 = (pred[768]{0:T(1024)(128)(4,1)}, pred[768]{0:T(1024)(128)(4,1)S(1)}, u32[]{:S(2)}) copy-start(pred[768]{0:T(1024)(128)(4,1)S(1)} %fusion.46) | copy-start | bytes 2308
  29.1 22.5 %copy-start.40 = (s32[768]{0:T(1024)}, s32[768]{0:T(1024)S(1)}, u32[]{:S(2)}) copy-start(s32[768]{0:T(1024)S(1)} %subtract_select_fusion) | copy-start | bytes 9220
  66.3 20.4 %copy-start.10 = (bf16[384,384]{1,0:T(8,128)(2,1)S(1)}, bf16[384,384]{1,0:T(8,128)(2,1)}, u32[]{:S(2)}) copy-start(bf16[384,384]{1,0:T(8,128)(2,1)} %fusion.64) | copy-start | bytes 884740
  66.3 20.4 %copy-start.11 = (bf16[384,384]{1,0:T(8,128)(2,1)S(1)}, bf16[384,384]{1,0:T(8,128)(2,1)}, u32[]{:S(2)}) copy-start(bf16[384,384]{1,0:T(8,128)(2,1)} %get-tuple-element.37) | copy-start | bytes 884740
  75.2 14.8 %copy-start.3 = (bf16[12,48,384]{2,1,0:T(8,128)(2,1)S(1)}, bf16[12,48,384]{2,1,0:T(8,128)(2,1)}, u32[]{:S(2)}) copy-start(bf16[12,48,384]{2,1,0:T(8,128)(2,1)} %param.7) | copy-start | bytes 1327108
  75.2 26.7 %all-to-all-start.1 = ((bf16[32,2,3456]{2,1,0:T(2,128)(2,1)}), bf16[32,2,3456]{2,1,0:T(2,128)(2,1)S(1)}, u32[]{:S(2)}, u32[]{:S(2)}) async-start(bf16[32,2,3456]{2,1,0:T(2,128)(2,1)} %reshape.465), calls=%async_computation.1 | async-start | bytes 884736 | tf_op jit(solution)/shard_map/all_to_all | solution.py:82
  90.0 8.1 %copy-start.13 = (bf16[12,2,384]{2,1,0:T(2,128)(2,1)}, bf16[12,2,384]{2,1,0:T(2,128)(2,1)S(1)}, u32[]{:S(2)}) copy-start(bf16[12,2,384]{2,1,0:T(2,128)(2,1)S(1)} %collective-permute-done) | copy-start | bytes 55300
  90.0 8.1 %copy-start.15 = (bf16[12,2,384]{2,1,0:T(2,128)(2,1)}, bf16[12,2,384]{2,1,0:T(2,128)(2,1)S(1)}, u32[]{:S(2)}) copy-start(bf16[12,2,384]{2,1,0:T(2,128)(2,1)S(1)} %collective-permute-done.1) | copy-start | bytes 55300
  90.9 33.8 %collective-permute-start.2 = (bf16[2,52,384]{2,1,0:T(8,128)(2,1)}, bf16[2,52,384]{2,1,0:T(8,128)(2,1)}, u32[]{:S(2)}, u32[]{:S(2)}) collective-permute-start(bf16[2,52,384]{2,1,0:T(8,128)(2,1)} %get-tuple-element.39), channel_id=1, source_target_pairs={{0,16},{16,32},{32,48},{48,64},{64,80},{80,96},{96,112},{112,128},... | collective-permute-start | bytes 239624 | tf_op jit(solution)/shard_map/ppermute | solution.py:20
  94.7 30.0 %collective-permute-start.3 = (bf16[2,52,384]{2,1,0:T(8,128)(2,1)}, bf16[2,52,384]{2,1,0:T(8,128)(2,1)}, u32[]{:S(2)}, u32[]{:S(2)}) collective-permute-start(bf16[2,52,384]{2,1,0:T(8,128)(2,1)} %get-tuple-element.40), channel_id=1, source_target_pairs={{16,0},{32,16},{48,32},{64,48},{80,64},{96,80},{112,96},{128,112},... | collective-permute-start | bytes 239624 | tf_op jit(solution)/shard_map/ppermute | solution.py:22
  114.6 10.1 %copy-start.14 = (bf16[12,2,384]{2,1,0:T(2,128)(2,1)S(1)}, bf16[12,2,384]{2,1,0:T(2,128)(2,1)}, u32[]{:S(2)}) copy-start(bf16[12,2,384]{2,1,0:T(2,128)(2,1)} %copy-done.13) | copy-start | bytes 55300
  114.6 10.1 %copy-start.16 = (bf16[12,2,384]{2,1,0:T(2,128)(2,1)S(1)}, bf16[12,2,384]{2,1,0:T(2,128)(2,1)}, u32[]{:S(2)}) copy-start(bf16[12,2,384]{2,1,0:T(2,128)(2,1)} %copy-done.15) | copy-start | bytes 55300
  118.4 21.7 %all-to-all-start.2 = ((bf16[16,2,6912]{2,1,0:T(2,128)(2,1)}), bf16[16,2,6912]{2,1,0:T(2,128)(2,1)S(1)}, u32[]{:S(2)}, u32[]{:S(2)}) async-start(bf16[16,2,6912]{2,1,0:T(2,128)(2,1)} %reshape.467), calls=%async_computation.2 | async-start | bytes 884736 | tf_op jit(solution)/shard_map/all_to_all | solution.py:95
  172.1 17.6 %all-to-all-start.3 = ((bf16[16,2,6912]{2,1,0:T(2,128)(2,1)}), bf16[16,2,6912]{2,1,0:T(2,128)(2,1)S(1)}, u32[]{:S(2)}, u32[]{:S(2)}) async-start(bf16[16,2,6912]{2,1,0:T(2,128)(2,1)} %reshape.469), calls=%async_computation.3 | async-start | bytes 884736 | tf_op jit(solution)/shard_map/all_to_all | solution.py:99
  194.1 9.2 %copy-start.2 = (bf16[2,6,384,384]{2,3,0,1:T(8,128)(2,1)S(1)}, bf16[2,6,384,384]{2,3,0,1:T(8,128)(2,1)}, u32[]{:S(2)}) copy-start(bf16[2,6,384,384]{2,3,0,1:T(8,128)(2,1)} %all-gather.2.cloned.1.call-done) | copy-start | bytes 10616836
  206.6 14.9 %copy-start.5 = (f32[12,48,384]{2,1,0:T(8,128)S(1)}, f32[12,48,384]{2,1,0:T(8,128)}, u32[]{:S(2)}) copy-start(f32[12,48,384]{2,1,0:T(8,128)} %get-tuple-element.18) | copy-start | bytes 2654212
  206.6 14.9 %copy-start.19 = (f32[3,12]{1,0:T(4,128)S(1)}, f32[3,12]{1,0:T(4,128)}, u32[]{:S(2)}) copy-start(f32[3,12]{1,0:T(4,128)} %get-tuple-element.69) | copy-start | bytes 436
  206.6 14.9 %copy-start.20 = (f32[3,12]{1,0:T(4,128)S(1)}, f32[3,12]{1,0:T(4,128)}, u32[]{:S(2)}) copy-start(f32[3,12]{1,0:T(4,128)} %get-tuple-element.70) | copy-start | bytes 436
  206.6 14.9 %copy-start.21 = (f32[3,12]{1,0:T(4,128)S(1)}, f32[3,12]{1,0:T(4,128)}, u32[]{:S(2)}) copy-start(f32[3,12]{1,0:T(4,128)} %get-tuple-element.71) | copy-start | bytes 436
  206.6 14.9 %copy-start.22 = (f32[3,12]{1,0:T(4,128)S(1)}, f32[3,12]{1,0:T(4,128)}, u32[]{:S(2)}) copy-start(f32[3,12]{1,0:T(4,128)} %get-tuple-element.47) | copy-start | bytes 436
  206.6 14.9 %copy-start.23 = (f32[3,12]{1,0:T(4,128)S(1)}, f32[3,12]{1,0:T(4,128)}, u32[]{:S(2)}) copy-start(f32[3,12]{1,0:T(4,128)} %get-tuple-element.48) | copy-start | bytes 436
  206.6 14.9 %copy-start.24 = (f32[3,12]{1,0:T(4,128)S(1)}, f32[3,12]{1,0:T(4,128)}, u32[]{:S(2)}) copy-start(f32[3,12]{1,0:T(4,128)} %get-tuple-element.49) | copy-start | bytes 436
  206.6 14.9 %copy-start.25 = (f32[3,12]{1,0:T(4,128)S(1)}, f32[3,12]{1,0:T(4,128)}, u32[]{:S(2)}) copy-start(f32[3,12]{1,0:T(4,128)} %get-tuple-element.50) | copy-start | bytes 436
  206.6 14.9 %copy-start.26 = (f32[3,12]{1,0:T(4,128)S(1)}, f32[3,12]{1,0:T(4,128)}, u32[]{:S(2)}) copy-start(f32[3,12]{1,0:T(4,128)} %get-tuple-element.51) | copy-start | bytes 436
  206.6 14.9 %copy-start.27 = (f32[3,12]{1,0:T(4,128)S(1)}, f32[3,12]{1,0:T(4,128)}, u32[]{:S(2)}) copy-start(f32[3,12]{1,0:T(4,128)} %get-tuple-element.52) | copy-start | bytes 436
  206.7 14.9 %copy-start.28 = (f32[3,12]{1,0:T(4,128)S(1)}, f32[3,12]{1,0:T(4,128)}, u32[]{:S(2)}) copy-start(f32[3,12]{1,0:T(4,128)} %get-tuple-element.53) | copy-start | bytes 436
  206.7 14.9 %copy-start.29 = (f32[3,12]{1,0:T(4,128)S(1)}, f32[3,12]{1,0:T(4,128)}, u32[]{:S(2)}) copy-start(f32[3,12]{1,0:T(4,128)} %get-tuple-element.54) | copy-start | bytes 436
  206.7 14.9 %copy-start.30 = (f32[3,12]{1,0:T(4,128)S(1)}, f32[3,12]{1,0:T(4,128)}, u32[]{:S(2)}) copy-start(f32[3,12]{1,0:T(4,128)} %get-tuple-element.55) | copy-start | bytes 436
  206.7 14.9 %copy-start.31 = (f32[3,12]{1,0:T(4,128)S(1)}, f32[3,12]{1,0:T(4,128)}, u32[]{:S(2)}) copy-start(f32[3,12]{1,0:T(4,128)} %get-tuple-element.56) | copy-start | bytes 436
  206.7 14.9 %copy-start.32 = (f32[3,12]{1,0:T(4,128)S(1)}, f32[3,12]{1,0:T(4,128)}, u32[]{:S(2)}) copy-start(f32[3,12]{1,0:T(4,128)} %get-tuple-element.57) | copy-start | bytes 436
  206.7 14.9 %copy-start.33 = (f32[3,12]{1,0:T(4,128)S(1)}, f32[3,12]{1,0:T(4,128)}, u32[]{:S(2)}) copy-start(f32[3,12]{1,0:T(4,128)} %get-tuple-element.58) | copy-start | bytes 436
  206.7 14.9 %copy-start.34 = (f32[3,12]{1,0:T(4,128)S(1)}, f32[3,12]{1,0:T(4,128)}, u32[]{:S(2)}) copy-start(f32[3,12]{1,0:T(4,128)} %get-tuple-element.59) | copy-start | bytes 436
  206.7 14.9 %copy-start.35 = (f32[3,12]{1,0:T(4,128)S(1)}, f32[3,12]{1,0:T(4,128)}, u32[]{:S(2)}) copy-start(f32[3,12]{1,0:T(4,128)} %get-tuple-element.60) | copy-start | bytes 436
  206.7 14.9 %copy-start.36 = (f32[3,12]{1,0:T(4,128)S(1)}, f32[3,12]{1,0:T(4,128)}, u32[]{:S(2)}) copy-start(f32[3,12]{1,0:T(4,128)} %get-tuple-element.61) | copy-start | bytes 436
  206.7 14.9 %copy-start.37 = (f32[3,12]{1,0:T(4,128)S(1)}, f32[3,12]{1,0:T(4,128)}, u32[]{:S(2)}) copy-start(f32[3,12]{1,0:T(4,128)} %get-tuple-element.62) | copy-start | bytes 436
  206.8 14.9 %copy-start.38 = (f32[3,12]{1,0:T(4,128)S(1)}, f32[3,12]{1,0:T(4,128)}, u32[]{:S(2)}) copy-start(f32[3,12]{1,0:T(4,128)} %get-tuple-element.63) | copy-start | bytes 436
  206.8 14.9 %copy-start.39 = (f32[3,12]{1,0:T(4,128)S(1)}, f32[3,12]{1,0:T(4,128)}, u32[]{:S(2)}) copy-start(f32[3,12]{1,0:T(4,128)} %get-tuple-element.64) | copy-start | bytes 436
  215.8 20.8 %all-to-all-start.4 = ((bf16[32,2,3456]{2,1,0:T(2,128)(2,1)}), bf16[32,2,3456]{2,1,0:T(2,128)(2,1)}, u32[]{:S(2)}, u32[]{:S(2)}) async-start(bf16[32,2,3456]{2,1,0:T(2,128)(2,1)} %reshape.471), calls=%async_computation.4 | async-start | bytes 884736 | tf_op jit(solution)/shard_map/all_to_all | solution.py:104
  245.2 5.8 %copy-start.41 = (s32[768]{0:T(1024)S(1)}, s32[768]{0:T(1024)}, u32[]{:S(2)}) copy-start(s32[768]{0:T(1024)} %copy-done.40) | copy-start | bytes 9220
  245.2 5.8 %copy-start.43 = (pred[768]{0:T(1024)(128)(4,1)S(1)}, pred[768]{0:T(1024)(128)(4,1)}, u32[]{:S(2)}) copy-start(pred[768]{0:T(1024)(128)(4,1)} %copy-done.42) | copy-start | bytes 2308
  269.8 7.6 %copy-start.8 = (bf16[1,12,48,384]{3,2,1,0:T(8,128)(2,1)S(1)}, bf16[1,12,48,384]{3,2,1,0:T(8,128)(2,1)}, u32[]{:S(2)}) copy-start(bf16[1,12,48,384]{3,2,1,0:T(8,128)(2,1)} %get-tuple-element.6) | copy-start | bytes 1327108
  269.8 7.6 %copy-start.12 = (bf16[3,384,384]{2,1,0:T(8,128)(2,1)S(1)}, bf16[3,384,384]{2,1,0:T(8,128)(2,1)}, u32[]{:S(2)}) copy-start(bf16[3,384,384]{2,1,0:T(8,128)(2,1)} %param.10) | copy-start | bytes 2654212
  269.8 8.0 %copy-start.7 = (bf16[1,12,48,384]{3,2,1,0:T(8,128)(2,1)S(1)}, bf16[1,12,48,384]{3,2,1,0:T(8,128)(2,1)}, u32[]{:S(2)}) copy-start(bf16[1,12,48,384]{3,2,1,0:T(8,128)(2,1)} %get-tuple-element.5) | copy-start | bytes 1327108
  269.8 21.8 %all-to-all-start.5 = ((bf16[16,2,6912]{2,1,0:T(2,128)(2,1)}), bf16[16,2,6912]{2,1,0:T(2,128)(2,1)}, u32[]{:S(2)}, u32[]{:S(2)}) async-start(bf16[16,2,6912]{2,1,0:T(2,128)(2,1)} %reshape.473), calls=%async_computation.5 | async-start | bytes 884736 | tf_op jit(solution)/shard_map/all_to_all | solution.py:109
  300.2 2.1 copy-start.4
  300.2 2.1 copy-start.6
  300.2 3.3 %copy-start.1 = (f32[384,384]{1,0:T(8,128)S(1)}, f32[384,384]{1,0:T(8,128)}, u32[]{:S(2)}) copy-start(f32[384,384]{1,0:T(8,128)} %param.13) | copy-start | bytes 1769476
Sparse Core Ops, SparseCore 0:
  9.4 57.3 all-gather.1
where the time goes:
time: 315 us; the launch traced here: 311 us
  local copies, waits for them, and re-layouts  139 us (44%)
  waiting for transfers between devices  54.4 us (17%)
  starting transfers between devices  52.1 us (17%)
  matrix products  32.6 us (10%)
  other arithmetic  18.5 us (6%)
  between operations  14.5 us (5%)
    unnamed x102, local copies, waits for them, and re-layouts  64.3 us
    unnamed x2, matrix products  20.6 us
    all_to_all x1, waiting for transfers between devices, on_device(): lax.all_to_all(grid_field, 'lon', split_axis=2, concat_axis=1, tiled=True)  16.1 us
    all_to_all x1, waiting for transfers between devices, on_device(): lax.all_to_all(spectral, 'lon', split_axis=1, concat_axis=2, tiled=True)  12.4 us
    all_to_all x1, waiting for transfers between devices, on_device(): lax.all_to_all(spectrum, 'lon', split_axis=2, concat_axis=4, tiled=True)  11.9 us
    all_to_all x1, starting transfers between devices, on_device(): lax.all_to_all(fourier, 'lat', split_axis=1, concat_axis=0, tiled=True)  11.5 us
    convert_element_type x1, other arithmetic, on_device(): summed.astype(jnp.bfloat16)  11.2 us
    slice x5, local copies, waits for them, and re-layouts, on_device(): summed = summed + column_sum[:, :, col_step:col_step + lon_dev]  10.6 us
  transfers between devices with their start and end apart: 11, of which 6 were waited for; matrix products, arithmetic and copies ran while one was open for 27% of the time, Pallas kernels for 0%

commit v1 on v0

v1 whole, which is shorter than its diff:
```python
import math

import jax
import jax.numpy as jnp
import numpy as np
from jax import lax
from jax.experimental import pallas as pl
from jax.experimental.pallas import tpu as pltpu
from jax.sharding import PartitionSpec as P

C = 384
NLAT = 384
NLON = 768
MMAX = 384
LMAX = 384
KERNELS = 3
LAT = 32
LON = 16
BAND = NLAT // LAT
TILE = NLON // LON
MS = 12
LEG = NLAT // LON
CHUNKS = 3
CW = C // CHUNKS
MESH = pl.DeviceIdType.MESH


def constant_tables():
    group = np.arange(LAT)[:, None, None, None]
    half = np.arange(2)[None, :, None, None]
    pair = np.arange(6)[None, None, :, None]
    index = group * 6 + pair
    wavenumber = np.where(half == 0, index, MMAX - 1 - index) + np.zeros((1, 1, 1, 2), np.int64)
    component = np.zeros_like(wavenumber) + np.arange(2)
    wavenumber = wavenumber.reshape(-1)
    component = component.reshape(-1)
    phases = (wavenumber[:, None] * np.arange(NLON)[None, :]) % NLON
    angles = phases.astype(np.float32) * np.float32(2.0 * math.pi / NLON)
    values = np.where(component[:, None] == 0, np.cos(angles), -np.sin(angles))
    values = values.astype(np.float32) * np.float32(1.0 / math.sqrt(NLON))
    table = jnp.asarray(values, jnp.bfloat16)
    table_t = jnp.asarray(values.T.copy(), jnp.bfloat16)
    perm = np.zeros((2 * MMAX, 2 * MMAX), np.float32)
    for band in range(LAT):
        for inner in range(2 * MS):
            perm[inner * LAT + band, band * 2 * MS + inner] = 1.0
    perm_leg = np.zeros((NLAT, NLAT), np.float32)
    for t in range(NLAT):
        perm_leg[(t % BAND) * LAT + t // BAND, t] = 1.0
    return (
        table,
        table_t,
        jnp.asarray(perm, jnp.bfloat16),
        jnp.asarray(perm.T.copy(), jnp.bfloat16),
        jnp.asarray(perm_leg, jnp.bfloat16),
    )


def dot(a, b):
    return jnp.dot(a, b, preferred_element_type=jnp.float32)


def kernel(
    grid_hbm, filt, offs, dw_hbm, leg_hbm, sw_hbm, gain_hbm, tab_hbm, tabt_hbm, pf_hbm, pb_hbm, pl_hbm,
    out_ref,
    grid_v, pad, dw, sw, gain, tab, tabt, pf, pb, pleg,
    legrecv, legp, legn, rows, fsend, frecv, gsend, hrecv, spec, rsend, gback, bsend, ret, ssend, srecv,
    basis, disco,
    load_sem, x1_send, x1_recv, leg_send, leg_recv, halo_send, halo_recv,
    a_send, a_recv, b_send, b_recv, c_send, c_recv, d_send, d_recv, e_send, e_recv,
):
    bf16 = jnp.bfloat16
    f32 = jnp.float32
    lat = lax.axis_index("lat")
    lon = lax.axis_index("lon")
    quad = lax.div(lon, 4)
    place = lax.rem(lon, 4)
    active = place < 3
    mine = quad * 3 + jnp.minimum(place, 2)

    north = lax.rem(lat + LAT - 1, LAT)
    south = lax.rem(lat + 1, LAT)
    west = lax.rem(lon + LON - 1, LON)
    east = lax.rem(lon + 1, LON)

    loads = [
        pltpu.make_async_copy(src, dst, load_sem.at[n])
        for n, (src, dst) in enumerate(
            (
                (grid_hbm, grid_v), (tab_hbm, tab), (pf_hbm, pf), (pl_hbm, pleg),
                (dw_hbm, dw), (sw_hbm, sw), (gain_hbm, gain), (pb_hbm, pb), (tabt_hbm, tabt),
            )
        )
    ]
    load_grid, load_tab, load_pf, load_pleg, load_dw, load_sw, load_gain, load_pb, load_tabt = loads
    for load in loads:
        load.start()

    barrier = pltpu.get_barrier_semaphore()

    def greet(device):
        pl.semaphore_signal(barrier, inc=1, device_id=device, device_id_type=MESH)

    @pl.loop(1, LON)
    def _(d):
        greet((lat, lax.rem(lon + d, LON)))

    @pl.loop(1, LAT)
    def _(d):
        greet((lax.rem(lat + d, LAT), lon))

    for a in (north, south):
        for b in (west, east):
            greet((a, b))
    pl.semaphore_wait(barrier, LON - 1 + LAT - 1 + 4)

    def owner(row):
        return row + lax.div(row, 3)

    def remote(src, dst, send, recv, device):
        return pltpu.make_async_remote_copy(
            src_ref=src, dst_ref=dst, send_sem=send, recv_sem=recv, device_id=device, device_id_type=MESH
        )

    def to_rows(source, target, send, recv):
        @pl.loop(0, BAND)
        def _(d):
            row = lax.rem(mine + d, BAND)
            there = owner(row)

            @pl.when(there != lon)
            def _():
                remote(source(row), target, send, recv, (lat, there)).start()

            @pl.when(there == lon)
            def _():
                pltpu.make_async_copy(source(row), target, recv).start()

    def to_bands(source, target, send, recv):
        @pl.loop(1, LAT)
        def _(d):
            there = lax.rem(lat + d, LAT)
            remote(source(there), target, send, recv, (there, lon)).start()

        pltpu.make_async_copy(source(lat), target, recv).start()

    def wait(ref, sem):
        pltpu.make_async_copy(ref, ref, sem).wait()

    for ch in range(CHUNKS):
        to_rows(
            lambda row: grid_hbm.at[row, :, pl.ds(ch * CW, CW)], rows.at[ch, lon], x1_send, x1_recv.at[ch]
        )

    load_grid.wait()
    for ct in range(C // 128):
        pad[ct, 2 : 2 + BAND, 8 : 8 + TILE, :] = grid_v[:, :, ct * 128 : (ct + 1) * 128].astype(f32)
    n0, n1 = 8, 8 + TILE
    t0, t1 = 2, 2 + BAND
    halo = [
        remote(
            pad.at[:, pl.ds(sr, nr), pl.ds(sc, nc), :], pad.at[:, pl.ds(dr, nr), pl.ds(dc, nc), :],
            halo_send.at[n], halo_recv.at[n], device,
        )
        for n, (sr, nr, sc, nc, dr, dc, device) in enumerate(
            (
                (t0, BAND, n0, 8, t0, n1, (lat, west)),
                (t0, BAND, n1 - 8, 8, t0, 0, (lat, east)),
                (t0, 2, n0, TILE, t1, n0, (north, lon)),
                (t1 - 2, 2, n0, TILE, 0, n0, (south, lon)),
                (t0, 2, n0, 8, t1, n1, (north, west)),
                (t0, 2, n1 - 8, 8, t1, 0, (north, east)),
                (t1 - 2, 2, n0, 8, 0, n1, (south, west)),
                (t1 - 2, 2, n1 - 8, 8, 0, 0, (south, east)),
            )
        )
    ]
    for copy in halo:
        copy.start()

    to_rows(lambda row: leg_hbm.at[row], legrecv.at[lon], leg_send, leg_recv)

    load_tab.wait()
    load_pf.wait()
    load_pleg.wait()

    @pl.when(active)
    def _():
        for ch in range(CHUNKS):
            wait(rows.at[ch], x1_recv.at[ch])

            @pl.loop(0, 4)
            def _(b):
                part = dot(tab[pl.ds(b * 192, 192), :], rows[ch].reshape(NLON, CW))
                fsend[ch, pl.ds(b * 8, 8)] = part.reshape(8, 2 * MS, CW).astype(bf16)

            to_bands(lambda q: fsend.at[ch, q], frecv.at[ch, lat], a_send, a_recv.at[ch])

        wait(legrecv, leg_recv)
        shards = legrecv[...].astype(f32).reshape(NLAT, LMAX).astype(bf16)
        ordered = dot(pleg[...], shards)
        legp[...] = ordered.astype(bf16)
        legn[...] = ordered.T.astype(bf16)

        for ch in range(CHUNKS):
            wait(frecv.at[ch], a_recv.at[ch])

            @pl.loop(0, 4)
            def _(b):
                got = frecv[ch].astype(f32).reshape(2 * MMAX, CW).astype(bf16)
                part = dot(pf[pl.ds(b * 192, 192), :], got)
                gsend[ch, pl.ds(b * 3, 3)] = part.reshape(3, 2 * LAT, CW).astype(bf16)

            to_rows(lambda m: gsend.at[ch, m], hrecv.at[ch, mine], b_send, b_recv.at[ch])

    load_dw.wait()
    for copy in halo:
        copy.wait_recv()

    @pl.loop(0, BAND)
    def _(i):
        for k in range(KERNELS):
            totals = [jnp.zeros((TILE, 128), f32)] * (C // 128)
            for j in range(5):
                t = lat * BAND + i + (j - 2)
                inside = jnp.logical_and(t >= 0, t < NLAT)
                scale = jnp.where(inside, filt[k, j, i], 0.0)
                first = 8 + offs[k, j, i]
                totals = [
                    total + scale * pad[ct, i + j, pl.ds(first, TILE), :] for ct, total in enumerate(totals)
                ]
            for ct, total in enumerate(totals):
                at = k * C + ct * 128
                basis[pl.ds(i * TILE, TILE), at : at + 128] = total.astype(bf16)

    @pl.loop(0, 4)
    def _(b):
        disco[pl.ds(b * 144, 144), :] = dot(basis[pl.ds(b * 144, 144), :], dw[...])

    load_sw.wait()
    load_gain.wait()
    load_pb.wait()
    load_tabt.wait()

    @pl.when(active)
    def _():
        for ch in range(CHUNKS):
            wait(hrecv.at[ch], b_recv.at[ch])
            for r in range(2):
                part = hrecv[ch, :, r * LAT : (r + 1) * LAT, :].reshape(NLAT, CW)
                spec[:, r * C + ch * CW : r * C + (ch + 1) * CW] = dot(legn[...], part).astype(bf16)

        for ch in range(CHUNKS):
            cols = slice(ch * CW, (ch + 1) * CW)
            re = spec[:, :C]
            im = spec[:, C:]
            filtered = (
                dot(re, sw[0, :, cols]) - dot(im, sw[1, :, cols]),
                dot(re, sw[1, :, cols]) + dot(im, sw[0, :, cols]),
            )
            for r in range(2):
                value = (filtered[r] * gain[:, cols]).astype(bf16)
                back = dot(legp[...], value)
                rsend[ch, :, r * LAT : (r + 1) * LAT, :] = back.astype(bf16).reshape(BAND, LAT, CW)
            to_rows(lambda row: rsend.at[ch, row], gback.at[ch, mine], c_send, c_recv.at[ch])

        for ch in range(CHUNKS):
            wait(gback.at[ch], c_recv.at[ch])

            @pl.loop(0, 4)
            def _(b):
                part = dot(pb[pl.ds(b * 192, 192), :], gback[ch].reshape(2 * MMAX, CW))
                bsend[ch, pl.ds(b * 8, 8)] = part.reshape(8, 2 * MS, CW).astype(bf16)

            to_bands(lambda q: bsend.at[ch, q], ret.at[ch, lat], d_send, d_recv.at[ch])

        for ch in range(CHUNKS):
            wait(ret.at[ch], d_recv.at[ch])

            @pl.loop(0, 4)
            def _(b):
                got = ret[ch].astype(f32).reshape(2 * MMAX, CW).astype(bf16)
                part = dot(tabt[pl.ds(b * 192, 192), :], got)
                ssend[ch, pl.ds(b * 4, 4)] = part.reshape(4, TILE, CW).astype(bf16)

            @pl.loop(1, LON)
            def _(d):
                there = lax.rem(lon + d, LON)
                remote(
                    ssend.at[ch, there], srecv.at[ch, mine], e_send, e_recv.at[ch], (lat, there)
                ).start()

            pltpu.make_async_copy(ssend.at[ch, lon], srecv.at[ch, mine], e_recv.at[ch]).start()

    for ch in range(CHUNKS):
        cols = slice(ch * CW, (ch + 1) * CW)
        wait(srecv.at[ch], e_recv.at[ch])

        @pl.loop(0, BAND)
        def _(i):
            combined = srecv[ch, i].astype(f32) + disco[pl.ds(i * TILE, TILE), cols]
            out_ref[i, :, cols] = (grid_v[i, :, cols].astype(f32) + jax.nn.gelu(combined)).astype(bf16)

    for copy in halo:
        copy.wait_send()

    @pl.when(active)
    def _():
        wait(rows.at[:, pl.ds(0, BAND - 1)], x1_send)
        wait(legrecv.at[pl.ds(0, MS - 1)], leg_send)
        wait(fsend.at[:, pl.ds(0, LAT - 1)], a_send)
        wait(gsend.at[:, pl.ds(0, MS - 1)], b_send)
        wait(rsend.at[:, pl.ds(0, BAND - 1)], c_send)
        wait(bsend.at[:, pl.ds(0, LAT - 1)], d_send)
        wait(ssend.at[:, pl.ds(0, LON - 1)], e_send)

    @pl.when(jnp.logical_not(active))
    def _():
        wait(rows.at[:, pl.ds(0, BAND)], x1_send)
        wait(legrecv.at[pl.ds(0, MS)], leg_send)


def on_device(grid_field, disco_filter, offsets, disco_weight, legendre, spec_weight, degree_gain):
    bf16 = jnp.bfloat16
    f32 = jnp.float32
    smem = pl.BlockSpec(memory_space=pltpu.SMEM)
    hbm = pl.BlockSpec(memory_space=pl.ANY)
    dma = pltpu.SemaphoreType.DMA
    vmem = pltpu.VMEM
    return pl.pallas_call(
        kernel,
        out_shape=jax.ShapeDtypeStruct(grid_field.shape, bf16),
        in_specs=[hbm, smem, smem] + [hbm] * 9,
        out_specs=pl.BlockSpec(memory_space=pltpu.VMEM),
        scratch_shapes=[
            vmem((BAND, TILE, C), bf16),
            vmem((C // 128, BAND + 4, TILE + 16, 128), f32),
            vmem((KERNELS * C, C), bf16),
            vmem((2, C, C), bf16),
            vmem((LMAX, C), f32),
            vmem((2 * MMAX, NLON), bf16),
            vmem((NLON, 2 * MMAX), bf16),
            vmem((2 * MMAX, 2 * MMAX), bf16),
            vmem((2 * MMAX, 2 * MMAX), bf16),
            vmem((NLAT, NLAT), bf16),
            vmem((LON, LEG, LMAX), bf16),
            vmem((NLAT, LMAX), bf16),
            vmem((LMAX, NLAT), bf16),
            vmem((CHUNKS, LON, TILE, CW), bf16),
            vmem((CHUNKS, LAT, 2 * MS, CW), bf16),
            vmem((CHUNKS, LAT, 2 * MS, CW), bf16),
            vmem((CHUNKS, MS, 2 * LAT, CW), bf16),
            vmem((CHUNKS, BAND, 2 * LAT, CW), bf16),
            vmem((LMAX, 2 * C), bf16),
            vmem((CHUNKS, BAND, 2 * LAT, CW), bf16),
            vmem((CHUNKS, MS, 2 * LAT, CW), bf16),
            vmem((CHUNKS, LAT, 2 * MS, CW), bf16),
            vmem((CHUNKS, LAT, 2 * MS, CW), bf16),
            vmem((CHUNKS, LON, TILE, CW), bf16),
            vmem((CHUNKS, BAND, TILE, CW), bf16),
            vmem((BAND * TILE, KERNELS * C), bf16),
            vmem((BAND * TILE, C), f32),
            dma((9,)),
            dma, dma((CHUNKS,)),
            dma, dma,
            dma((8,)), dma((8,)),
            dma, dma((CHUNKS,)),
            dma, dma((CHUNKS,)),
            dma, dma((CHUNKS,)),
            dma, dma((CHUNKS,)),
            dma, dma((CHUNKS,)),
        ],
        compiler_params=pltpu.CompilerParams(
            collective_id=0, has_side_effects=True, vmem_limit_bytes=48 * 1024 * 1024
        ),
        cost_estimate=pl.CostEstimate(flops=3_000_000_000, bytes_accessed=8_000_000, transcendentals=221_184),
    )(
        grid_field,
        disco_filter,
        offsets,
        disco_weight.reshape(KERNELS * C, C),
        jnp.swapaxes(legendre.reshape(MS, LMAX, LEG), 1, 2),
        spec_weight,
        degree_gain,
        *constant_tables(),
    )


def solution(mesh):
    in_specs = (
        P("lat", "lon", None),
        P(None, None, "lat"),
        P(None, None, "lat"),
        P(),
        P(None, "lat", None, "lon"),
        P(),
        P(),
    )
    out_specs = P("lat", "lon", None)
    return jax.shard_map(
        on_device, mesh=mesh, in_specs=in_specs, out_specs=out_specs, check_vma=False
    )
```

time: 315 us -> 101 us (0.32); the launches traced: 311 us -> 101 us
  local copies, waits for them, and re-layouts: 139 us -> 10.9 us
  Pallas kernels: 0 us -> 89.8 us
  waiting for transfers between devices: 54.4 us -> 0 us
  starting transfers between devices: 52.1 us -> 0 us
  matrix products: 32.6 us -> 0 us
  other arithmetic: 18.5 us -> 0 us
  between operations: 14.5 us -> 0.02 us
    pallas_call x0 -> x1, Pallas kernels: none -> 89.8 us  [on_device(): pl.pallas_call(kernel, out_shape=jax.ShapeDtypeStruct(grid_field.shape, b...]
    all_to_all x6 -> x0, waiting for transfers between devices: 54.3 us -> none  [the longest x1 16.1 us: on_device(): lax.all_to_all(grid_field, 'lon', split_axis=2, concat_axis=1, tiled=True)]
    unnamed x102 -> x19, local copies, waits for them, and re-layouts: 64.3 us -> 10.9 us
    all_to_all x6 -> x0, starting transfers between devices: 40.2 us -> none  [the longest x1 11.5 us: on_device(): lax.all_to_all(fourier, 'lat', split_axis=1, concat_axis=0, tiled=True)]
    convert_element_type x7 -> x0, local copies, waits for them, and re-layouts: 24.3 us -> none  [the longest x1 6.2 us: channel_mix(): return (mixed_rows * row_gain).astype(jnp.bfloat16)]
    all_to_all x7 -> x0, local copies, waits for them, and re-layouts: 24 us -> none  [the longest x2 9.19 us: on_device(): lax.all_to_all(filtered_part, 'lon', split_axis=4, concat_axis=2, tiled=T...]
    unnamed x2 -> x0, matrix products: 20.6 us -> none
    convert_element_type x6 -> x0, other arithmetic: 13.6 us -> none  [the longest x1 11.2 us: on_device(): summed.astype(jnp.bfloat16)]
  transfers between devices with their start and end apart: 11 -> 0, of which waited for: 6 -> 0; matrix products, arithmetic and copies ran while one was open for 27% -> 0% of each run, Pallas kernels for 0% -> 0%
where the time goes in v1:
time: 101 us
  Pallas kernels  89.8 us (89%)
  local copies, waits for them, and re-layouts  10.9 us (11%)
    pallas_call x1, Pallas kernels, on_device(): pl.pallas_call(kernel, out_shape=jax.ShapeDtypeStruct(grid_field.shape, b...  89.8 us
    unnamed x19, local copies, waits for them, and re-layouts  10.9 us

profile of v1, /device:TPU:1, one launch (start us, length us, event | category | flops | bytes accessed | tf_op | source)
XLA Modules:
  0.0 100.7 jit_solution(4754673262585567911)
XLA Ops:
  0.0 0.7 copy.13.filt
  0.7 0.7 copy.14.offs
  1.4 0.0 copy-start
  1.4 1.2 %copy-done = bf16[3,384,384]{2,1,0:T(8,128)(2,1)S(1)} copy-done((bf16[3,384,384]{2,1,0:T(8,128)(2,1)S(1)}, bf16[3,384,384]{2,1,0:T(8,128)(2,1)}, u32[]{:S(2)}) %copy-start) | copy-done | bytes 884760
  2.6 0.0 copy-start.1
  2.6 1.1 %copy-done.1 = bf16[2,384,384]{2,1,0:T(8,128)(2,1)S(1)} copy-done((bf16[2,384,384]{2,1,0:T(8,128)(2,1)S(1)}, bf16[2,384,384]{2,1,0:T(8,128)(2,1)}, u32[]{:S(2)}) %copy-start.1) | copy-done | bytes 589848
  3.6 0.0 copy-start.2
  3.6 1.1 %copy-done.2 = f32[384,384]{1,0:T(8,128)S(1)} copy-done((f32[384,384]{1,0:T(8,128)S(1)}, f32[384,384]{1,0:T(8,128)}, u32[]{:S(2)}) %copy-start.2) | copy-done | bytes 589848
  4.7 0.0 copy-start.3
  4.7 1.0 %copy-done.3 = bf16[12,48,384]{2,1,0:T(8,128)(2,1)S(1)} copy-done((bf16[12,48,384]{2,1,0:T(8,128)(2,1)S(1)}, bf16[12,48,384]{2,1,0:T(8,128)(2,1)}, u32[]{:S(2)}) %copy-start.3) | copy-done | bytes 442392
  5.7 0.0 copy-start.4
  5.7 0.9 copy-done.4
  6.7 0.0 copy-start.5
  6.7 1.3 %copy-done.5 = bf16[768,768]{1,0:T(8,128)(2,1)S(1)} copy-done((bf16[768,768]{1,0:T(8,128)(2,1)S(1)}, bf16[768,768]{1,0:T(8,128)(2,1)}, u32[]{:S(2)}) %copy-start.5) | copy-done | bytes 1179672
  7.9 0.0 copy-start.6
  7.9 1.3 %copy-done.6 = bf16[768,768]{1,0:T(8,128)(2,1)S(1)} copy-done((bf16[768,768]{1,0:T(8,128)(2,1)S(1)}, bf16[768,768]{1,0:T(8,128)(2,1)}, u32[]{:S(2)}) %copy-start.6) | copy-done | bytes 1179672
  9.2 0.0 copy-start.7
  9.2 1.0 copy-done.7
  10.2 89.8 %shard_map.118 = bf16[12,48,384]{2,1,0:T(8,128)(2,1)S(1)} custom-call(bf16[12,48,384]{2,1,0:T(8,128)(2,1)S(1)} %copy-done.3, f32[3,5,12]{2,1,0:T(8,128)S(1)} %copy.13.filt, s32[3,5,12]{2,1,0:T(8,128)S(1)} %copy.14.offs, bf16[1152,384]{1,0:T(8,128)(2,1)S(1)} %bitcast.4, bf16[12,24,384]{2,1,0:T(8,128)(2,1)S(1)} %bitcast.5, bf16[2,384,384]{2,1,0:T(8,128)(2,1)S(1)} %copy-done.1, ...), custom_call_target="tpu_custom_call" | custom-call | flops 3000000000 | bytes 8000000 | tf_op jit(solution)/shard_map/pallas_call | solution.py:330
  99.9 0.8 copy.16
Async XLA Ops:
  1.4 1.2 %copy-start = (bf16[3,384,384]{2,1,0:T(8,128)(2,1)S(1)}, bf16[3,384,384]{2,1,0:T(8,128)(2,1)}, u32[]{:S(2)}) copy-start(bf16[3,384,384]{2,1,0:T(8,128)(2,1)} %param.15) | copy-start | bytes 2654212
  2.6 1.1 %copy-start.1 = (bf16[2,384,384]{2,1,0:T(8,128)(2,1)S(1)}, bf16[2,384,384]{2,1,0:T(8,128)(2,1)}, u32[]{:S(2)}) copy-start(bf16[2,384,384]{2,1,0:T(8,128)(2,1)} %sw_hbm.1) | copy-start | bytes 1769476
  3.6 1.1 %copy-start.2 = (f32[384,384]{1,0:T(8,128)S(1)}, f32[384,384]{1,0:T(8,128)}, u32[]{:S(2)}) copy-start(f32[384,384]{1,0:T(8,128)} %gain_hbm.1) | copy-start | bytes 1769476
  4.7 1.0 %copy-start.3 = (bf16[12,48,384]{2,1,0:T(8,128)(2,1)S(1)}, bf16[12,48,384]{2,1,0:T(8,128)(2,1)}, u32[]{:S(2)}) copy-start(bf16[12,48,384]{2,1,0:T(8,128)(2,1)} %grid_hbm.1) | copy-start | bytes 1327108
  5.7 0.9 copy-start.4
  6.7 1.3 %copy-start.5 = (bf16[768,768]{1,0:T(8,128)(2,1)S(1)}, bf16[768,768]{1,0:T(8,128)(2,1)}, u32[]{:S(2)}) copy-start(bf16[768,768]{1,0:T(8,128)(2,1)} %constant.11.clone.tabt_hbm) | copy-start | bytes 3538948
  7.9 1.3 %copy-start.6 = (bf16[768,768]{1,0:T(8,128)(2,1)S(1)}, bf16[768,768]{1,0:T(8,128)(2,1)}, u32[]{:S(2)}) copy-start(bf16[768,768]{1,0:T(8,128)(2,1)} %constant.10.clone.tab_hbm) | copy-start | bytes 3538948
  9.2 1.0 copy-start.7

commit v2 on v1

--- a/solution.py
+++ b/solution.py
@@ -73,10 +73,29 @@
     f32 = jnp.float32
     lat = lax.axis_index("lat")
     lon = lax.axis_index("lon")
-    quad = lax.div(lon, 4)
-    place = lax.rem(lon, 4)
-    active = place < 3
-    mine = quad * 3 + jnp.minimum(place, 2)
+    y = lax.div(lon, 2)
+    z = lax.div(lat, 4)
+    x = lax.rem(lat, 4)
+
+    def has_row(device, ch):
+        return lax.rem(device, 4) != ch
+
+    def row_of(device, ch):
+        inner = lax.rem(device, 4)
+        return 3 * lax.div(device, 4) + jnp.where(inner > ch, inner - 1, inner)
+
+    def has_wavenumber(device):
+        inner = lax.rem(device, 8)
+        return jnp.logical_and(inner != 5, inner != 7)
+
+    def wavenumber_of(device):
+        return 6 * lax.div(device, 8) + jnp.minimum(lax.rem(device, 8), 5)
+
+    def ring(step):
+        near = 4 - lax.div(step + 1, 2)
+        return lax.rem(jnp.where(lax.rem(step, 2) == 0, 8 - near, near), 8)
+
+    my_wavenumber = wavenumber_of(lon)
 
     north = lax.rem(lat + LAT - 1, LAT)
     south = lax.rem(lat + 1, LAT)
@@ -114,33 +133,43 @@
             greet((a, b))
     pl.semaphore_wait(barrier, LON - 1 + LAT - 1 + 4)
 
-    def owner(row):
-        return row + lax.div(row, 3)
-
     def remote(src, dst, send, recv, device):
         return pltpu.make_async_remote_copy(
             src_ref=src, dst_ref=dst, send_sem=send, recv_sem=recv, device_id=device, device_id_type=MESH
         )
 
-    def to_rows(source, target, send, recv):
-        @pl.loop(0, BAND)
-        def _(d):
-            row = lax.rem(mine + d, BAND)
-            there = owner(row)
-
-            @pl.when(there != lon)
+    def along_lon(takes, number, source, target, send, recv):
+        @pl.loop(0, LON)
+        def _(step):
+            there = 2 * lax.rem(y + ring(lax.div(step, 2)), 8) + lax.rem(step, 2)
+            block = number(there)
+            taken = takes(there)
+
+            @pl.when(jnp.logical_and(taken, there != lon))
             def _():
-                remote(source(row), target, send, recv, (lat, there)).start()
-
-            @pl.when(there == lon)
+                remote(source(block), target, send, recv, (lat, there)).start()
+
+            @pl.when(jnp.logical_and(taken, there == lon))
             def _():
-                pltpu.make_async_copy(source(row), target, recv).start()
+                pltpu.make_async_copy(source(block), target, recv).start()
+
+    def to_rows(ch, source, target, send, recv):
+        along_lon(lambda d: has_row(d, ch), lambda d: row_of(d, ch), source, target, send, recv)
+
+    def to_wavenumbers(source, target, send, recv):
+        along_lon(has_wavenumber, wavenumber_of, source, target, send, recv)
+
+    def to_tiles(source, target, send, recv):
+        along_lon(lambda d: d >= 0, lambda d: d, source, target, send, recv)
 
     def to_bands(source, target, send, recv):
-        @pl.loop(1, LAT)
-        def _(d):
-            there = lax.rem(lat + d, LAT)
-            remote(source(there), target, send, recv, (there, lon)).start()
+        @pl.loop(0, LAT)
+        def _(step):
+            there = 4 * lax.rem(z + ring(lax.div(step, 4)), 8) + lax.rem(x + 2 + lax.rem(step, 4), 4)
+
+            @pl.when(there != lat)
+            def _():
+                remote(source(there), target, send, recv, (there, lon)).start()
 
         pltpu.make_async_copy(source(lat), target, recv).start()
 
@@ -149,7 +178,7 @@
 
     for ch in range(CHUNKS):
         to_rows(
-            lambda row: grid_hbm.at[row, :, pl.ds(ch * CW, CW)], rows.at[ch, lon], x1_send, x1_recv.at[ch]
+            ch, lambda row: grid_hbm.at[row, :, pl.ds(ch * CW, CW)], rows.at[ch, lon], x1_send.at[ch], x1_recv.at[ch]
         )
 
     load_grid.wait()
@@ -175,122 +204,141 @@
             )
         )
     ]
-    for copy in halo:
-        copy.start()
-
-    to_rows(lambda row: leg_hbm.at[row], legrecv.at[lon], leg_send, leg_recv)
-
-    load_tab.wait()
-    load_pf.wait()
-    load_pleg.wait()
-
-    @pl.when(active)
-    def _():
-        for ch in range(CHUNKS):
-            wait(rows.at[ch], x1_recv.at[ch])
-
-            @pl.loop(0, 4)
-            def _(b):
-                part = dot(tab[pl.ds(b * 192, 192), :], rows[ch].reshape(NLON, CW))
-                fsend[ch, pl.ds(b * 8, 8)] = part.reshape(8, 2 * MS, CW).astype(bf16)
-
-            to_bands(lambda q: fsend.at[ch, q], frecv.at[ch, lat], a_send, a_recv.at[ch])
-
+    def send_halo():
+        for copy in halo:
+            copy.start()
+
+    send_halo()
+
+    def send_legendre():
+        to_wavenumbers(lambda m: leg_hbm.at[m], legrecv.at[lon], leg_send, leg_recv)
+
+    def forward_fourier(ch):
+        wait(rows.at[ch], x1_recv.at[ch])
+
+        part = dot(tab[...], rows[ch].reshape(NLON, CW))
+        fsend[ch] = part.reshape(LAT, 2 * MS, CW).astype(bf16)
+
+    def send_a(ch):
+        to_bands(lambda q: fsend.at[ch, q], frecv.at[ch, lat], a_send.at[ch], a_recv.at[ch])
+
+    def order_legendre():
         wait(legrecv, leg_recv)
         shards = legrecv[...].astype(f32).reshape(NLAT, LMAX).astype(bf16)
         ordered = dot(pleg[...], shards)
         legp[...] = ordered.astype(bf16)
         legn[...] = ordered.T.astype(bf16)
 
-        for ch in range(CHUNKS):
-            wait(frecv.at[ch], a_recv.at[ch])
-
-            @pl.loop(0, 4)
-            def _(b):
-                got = frecv[ch].astype(f32).reshape(2 * MMAX, CW).astype(bf16)
-                part = dot(pf[pl.ds(b * 192, 192), :], got)
-                gsend[ch, pl.ds(b * 3, 3)] = part.reshape(3, 2 * LAT, CW).astype(bf16)
-
-            to_rows(lambda m: gsend.at[ch, m], hrecv.at[ch, mine], b_send, b_recv.at[ch])
+    def by_wavenumber(ch):
+        wait(frecv.at[ch], a_recv.at[ch])
+        got = frecv[ch].astype(f32).reshape(2 * MMAX, CW).astype(bf16)
+        gsend[ch] = dot(pf[...], got).reshape(MS, 2 * LAT, CW).astype(bf16)
+
+    def send_b(ch):
+        to_wavenumbers(lambda m: gsend.at[ch, m], hrecv.at[ch, row_of(lon, ch)], b_send.at[ch], b_recv.at[ch])
+
+    def stencil():
+        @pl.loop(0, BAND)
+        def _(i):
+            for k in range(KERNELS):
+                totals = [jnp.zeros((TILE, 128), f32)] * (C // 128)
+                for j in range(5):
+                    t = lat * BAND + i + (j - 2)
+                    inside = jnp.logical_and(t >= 0, t < NLAT)
+                    scale = jnp.where(inside, filt[j, k, i], 0.0)
+                    first = 8 + offs[j, k, i]
+                    totals = [
+                        total + scale * pad[ct, i + j, pl.ds(first, TILE), :] for ct, total in enumerate(totals)
+                    ]
+                for ct, total in enumerate(totals):
+                    at = k * C + ct * 128
+                    basis[pl.ds(i * TILE, TILE), at : at + 128] = total.astype(bf16)
+
+        @pl.loop(0, 4)
+        def _(b):
+            disco[pl.ds(b * 144, 144), :] = dot(basis[pl.ds(b * 144, 144), :], dw[...])
+
+    def legendre(ch):
+        wait(hrecv.at[ch], b_recv.at[ch])
+        for r in range(2):
+            part = hrecv[ch, :, r * LAT : (r + 1) * LAT, :].reshape(NLAT, CW)
+            spec[:, r * C + ch * CW : r * C + (ch + 1) * CW] = dot(legn[...], part).astype(bf16)
+
+    def mix_and_back(ch):
+        cols = slice(ch * CW, (ch + 1) * CW)
+        re = spec[:, :C]
+        im = spec[:, C:]
+        filtered = (
+            dot(re, sw[0, :, cols]) - dot(im, sw[1, :, cols]),
+            dot(re, sw[1, :, cols]) + dot(im, sw[0, :, cols]),
+        )
+        for r in range(2):
+            value = (filtered[r] * gain[:, cols]).astype(bf16)
+            back = dot(legp[...], value)
+            rsend[ch, :, r * LAT : (r + 1) * LAT, :] = back.astype(bf16).reshape(BAND, LAT, CW)
+
+    def send_c(ch):
+        to_rows(ch, lambda row: rsend.at[ch, row], gback.at[ch, my_wavenumber], c_send.at[ch], c_recv.at[ch])
+
+    def by_band(ch):
+        wait(gback.at[ch], c_recv.at[ch])
+
+        part = dot(pb[...], gback[ch].reshape(2 * MMAX, CW))
+        bsend[ch] = part.reshape(LAT, 2 * MS, CW).astype(bf16)
+
+    def send_d(ch):
+        to_bands(lambda q: bsend.at[ch, q], ret.at[ch, lat], d_send.at[ch], d_recv.at[ch])
+
+    def inverse_fourier(ch):
+        wait(ret.at[ch], d_recv.at[ch])
+        got = ret[ch].astype(f32).reshape(2 * MMAX, CW).astype(bf16)
+        ssend[ch] = dot(tabt[...], got).reshape(LON, TILE, CW).astype(bf16)
+
+    def send_e(ch):
+        to_tiles(lambda n: ssend.at[ch, n], srecv.at[ch, row_of(lon, ch)], e_send.at[ch], e_recv.at[ch])
+
+    def with_row(ch, step):
+        @pl.when(has_row(lon, ch))
+        def _():
+            step(ch)
+
+    def with_wavenumber(step):
+        @pl.when(has_wavenumber(lon))
+        def _():
+            step()
+
+    load_tab.wait()
+    send_legendre()
+    for ch in range(CHUNKS):
+        with_row(ch, lambda ch: (forward_fourier(ch), send_a(ch)))
+    load_pf.wait()
+    for ch in range(CHUNKS):
+        with_row(ch, lambda ch: (by_wavenumber(ch), send_b(ch)))
+
+    load_pleg.wait()
+    load_sw.wait()
+    load_gain.wait()
+    with_wavenumber(order_legendre)
 
     load_dw.wait()
+    load_pb.wait()
+    load_tabt.wait()
     for copy in halo:
         copy.wait_recv()
-
-    @pl.loop(0, BAND)
-    def _(i):
-        for k in range(KERNELS):
-            totals = [jnp.zeros((TILE, 128), f32)] * (C // 128)
-            for j in range(5):
-                t = lat * BAND + i + (j - 2)
-                inside = jnp.logical_and(t >= 0, t < NLAT)
-                scale = jnp.where(inside, filt[k, j, i], 0.0)
-                first = 8 + offs[k, j, i]
-                totals = [
-                    total + scale * pad[ct, i + j, pl.ds(first, TILE), :] for ct, total in enumerate(totals)
-                ]
-            for ct, total in enumerate(totals):
-                at = k * C + ct * 128
-                basis[pl.ds(i * TILE, TILE), at : at + 128] = total.astype(bf16)
-
-    @pl.loop(0, 4)
-    def _(b):
-        disco[pl.ds(b * 144, 144), :] = dot(basis[pl.ds(b * 144, 144), :], dw[...])
-
-    load_sw.wait()
-    load_gain.wait()
-    load_pb.wait()
-    load_tabt.wait()
-
-    @pl.when(active)
+    stencil()
+
+    @pl.when(has_wavenumber(lon))
     def _():
         for ch in range(CHUNKS):
-            wait(hrecv.at[ch], b_recv.at[ch])
-            for r in range(2):
-                part = hrecv[ch, :, r * LAT : (r + 1) * LAT, :].reshape(NLAT, CW)
-                spec[:, r * C + ch * CW : r * C + (ch + 1) * CW] = dot(legn[...], part).astype(bf16)
-
+            legendre(ch)
         for ch in range(CHUNKS):
-            cols = slice(ch * CW, (ch + 1) * CW)
-            re = spec[:, :C]
-            im = spec[:, C:]
-            filtered = (
-                dot(re, sw[0, :, cols]) - dot(im, sw[1, :, cols]),
-                dot(re, sw[1, :, cols]) + dot(im, sw[0, :, cols]),
-            )
-            for r in range(2):
-                value = (filtered[r] * gain[:, cols]).astype(bf16)
-                back = dot(legp[...], value)
-                rsend[ch, :, r * LAT : (r + 1) * LAT, :] = back.astype(bf16).reshape(BAND, LAT, CW)
-            to_rows(lambda row: rsend.at[ch, row], gback.at[ch, mine], c_send, c_recv.at[ch])
-
-        for ch in range(CHUNKS):
-            wait(gback.at[ch], c_recv.at[ch])
-
-            @pl.loop(0, 4)
-            def _(b):
-                part = dot(pb[pl.ds(b * 192, 192), :], gback[ch].reshape(2 * MMAX, CW))
-                bsend[ch, pl.ds(b * 8, 8)] = part.reshape(8, 2 * MS, CW).astype(bf16)
-
-            to_bands(lambda q: bsend.at[ch, q], ret.at[ch, lat], d_send, d_recv.at[ch])
-
-        for ch in range(CHUNKS):
-            wait(ret.at[ch], d_recv.at[ch])
-
-            @pl.loop(0, 4)
-            def _(b):
-                got = ret[ch].astype(f32).reshape(2 * MMAX, CW).astype(bf16)
-                part = dot(tabt[pl.ds(b * 192, 192), :], got)
-                ssend[ch, pl.ds(b * 4, 4)] = part.reshape(4, TILE, CW).astype(bf16)
-
-            @pl.loop(1, LON)
-            def _(d):
-                there = lax.rem(lon + d, LON)
-                remote(
-                    ssend.at[ch, there], srecv.at[ch, mine], e_send, e_recv.at[ch], (lat, there)
-                ).start()
-
-            pltpu.make_async_copy(ssend.at[ch, lon], srecv.at[ch, mine], e_recv.at[ch]).start()
+            mix_and_back(ch)
+            send_c(ch)
+
+    for ch in range(CHUNKS):
+        with_row(ch, lambda ch: (by_band(ch), send_d(ch)))
+    for ch in range(CHUNKS):
+        with_row(ch, lambda ch: (inverse_fourier(ch), send_e(ch)))
 
     for ch in range(CHUNKS):
         cols = slice(ch * CW, (ch + 1) * CW)
@@ -303,20 +351,39 @@
 
     for copy in halo:
         copy.wait_send()
-
-    @pl.when(active)
+    for ch in range(CHUNKS):
+        mine = has_row(lon, ch)
+
+        @pl.when(mine)
+        def _():
+            wait(rows.at[ch, pl.ds(0, BAND - 1)], x1_send.at[ch])
+            wait(fsend.at[ch, pl.ds(0, LAT - 1)], a_send.at[ch])
+            wait(bsend.at[ch, pl.ds(0, LAT - 1)], d_send.at[ch])
+            wait(ssend.at[ch, pl.ds(0, LON - 1)], e_send.at[ch])
+
+        @pl.when(jnp.logical_not(mine))
+        def _():
+            wait(rows.at[ch, pl.ds(0, BAND)], x1_send.at[ch])
+
+        @pl.when(jnp.logical_and(mine, has_wavenumber(lon)))
+        def _():
+            wait(gsend.at[ch, pl.ds(0, MS - 1)], b_send.at[ch])
+            wait(rsend.at[ch, pl.ds(0, BAND - 1)], c_send.at[ch])
+
+        @pl.when(jnp.logical_and(mine, jnp.logical_not(has_wavenumber(lon))))
+        def _():
+            wait(gsend.at[ch], b_send.at[ch])
+
+        @pl.when(jnp.logical_and(jnp.logical_not(mine), has_wavenumber(lon)))
+        def _():
+            wait(rsend.at[ch], c_send.at[ch])
+
+    @pl.when(has_wavenumber(lon))
     def _():
-        wait(rows.at[:, pl.ds(0, BAND - 1)], x1_send)
         wait(legrecv.at[pl.ds(0, MS - 1)], leg_send)
-        wait(fsend.at[:, pl.ds(0, LAT - 1)], a_send)
-        wait(gsend.at[:, pl.ds(0, MS - 1)], b_send)
-        wait(rsend.at[:, pl.ds(0, BAND - 1)], c_send)
-        wait(bsend.at[:, pl.ds(0, LAT - 1)], d_send)
-        wait(ssend.at[:, pl.ds(0, LON - 1)], e_send)
-
-    @pl.when(jnp.logical_not(active))
+
+    @pl.when(jnp.logical_not(has_wavenumber(lon)))
     def _():
-        wait(rows.at[:, pl.ds(0, BAND)], x1_send)
         wait(legrecv.at[pl.ds(0, MS)], leg_send)
 
 
@@ -324,7 +391,7 @@
     bf16 = jnp.bfloat16
     f32 = jnp.float32
     smem = pl.BlockSpec(memory_space=pltpu.SMEM)
-    hbm = pl.BlockSpec(memory_space=pl.ANY)
+    hbm = pl.BlockSpec(memory_space=pltpu.HBM)
     dma = pltpu.SemaphoreType.DMA
     vmem = pltpu.VMEM
     return pl.pallas_call(
@@ -361,23 +428,23 @@
             vmem((BAND * TILE, KERNELS * C), bf16),
             vmem((BAND * TILE, C), f32),
             dma((9,)),
-            dma, dma((CHUNKS,)),
+            dma((CHUNKS,)), dma((CHUNKS,)),
             dma, dma,
             dma((8,)), dma((8,)),
-            dma, dma((CHUNKS,)),
-            dma, dma((CHUNKS,)),
-            dma, dma((CHUNKS,)),
-            dma, dma((CHUNKS,)),
-            dma, dma((CHUNKS,)),
+            dma((CHUNKS,)), dma((CHUNKS,)),
+            dma((CHUNKS,)), dma((CHUNKS,)),
+            dma((CHUNKS,)), dma((CHUNKS,)),
+            dma((CHUNKS,)), dma((CHUNKS,)),
+            dma((CHUNKS,)), dma((CHUNKS,)),
         ],
         compiler_params=pltpu.CompilerParams(
-            collective_id=0, has_side_effects=True, vmem_limit_bytes=48 * 1024 * 1024
+            collective_id=0, has_side_effects=True, vmem_limit_bytes=62 * 1024 * 1024
         ),
         cost_estimate=pl.CostEstimate(flops=3_000_000_000, bytes_accessed=8_000_000, transcendentals=221_184),
     )(
         grid_field,
-        disco_filter,
-        offsets,
+        jnp.swapaxes(disco_filter, 0, 1),
+        jnp.swapaxes(offsets, 0, 1),
         disco_weight.reshape(KERNELS * C, C),
         jnp.swapaxes(legendre.reshape(MS, LMAX, LEG), 1, 2),
         spec_weight,

time: 101 us -> 83.9 us (0.83)
  local copies, waits for them, and re-layouts: 10.9 us -> 1.82 us
  Pallas kernels: 89.8 us -> 81.8 us
    unnamed x19 -> x1, local copies, waits for them, and re-layouts: 10.9 us -> 1.82 us
    pallas_call x1, Pallas kernels: 89.8 us -> 81.8 us  [on_device(): pl.pallas_call(kernel, out_shape=jax.ShapeDtypeStruct(grid_field.shape, b...]
where the time goes in v2:
time: 83.9 us; the launch traced here: 83.6 us
  Pallas kernels  81.8 us (97%)
  local copies, waits for them, and re-layouts  1.82 us (2%)
    pallas_call x1, Pallas kernels, on_device(): pl.pallas_call(kernel, out_shape=jax.ShapeDtypeStruct(grid_field.shape, b...  81.8 us
    unnamed x1, local copies, waits for them, and re-layouts  1.82 us

profile of v2, /device:TPU:1, one launch (start us, length us, event | category | flops | bytes accessed | tf_op | source)
XLA Modules:
  0.0 83.6 jit_solution(8714074618567280061)
XLA Ops:
  0.0 81.8 %shard_map.118 = bf16[12,48,384]{2,1,0:T(8,128)(2,1)} custom-call(bf16[12,48,384]{2,1,0:T(8,128)(2,1)} %grid_hbm.1, f32[5,3,12]{2,1,0:T(4,128)} %bitcast.8, s32[5,3,12]{2,1,0:T(4,128)} %bitcast.9, bf16[1152,384]{1,0:T(8,128)(2,1)} %bitcast.6, bf16[12,24,384]{2,1,0:T(8,128)(2,1)} %bitcast.7, bf16[2,384,384]{2,1,0:T(8,128)(2,1)} %sw_hbm.1, ...), custom_call_target="tpu_custom_call" | custom-call | flops 3000000000 | bytes 8000000 | tf_op jit(solution)/shard_map/pallas_call | solution.py:397
  81.8 1.8 %copy.14 = bf16[12,48,384]{2,1,0:T(8,128)(2,1)} copy(bf16[12,48,384]{2,1,0:T(8,128)(2,1)} %shard_map.118) | data formatting | bytes 884736

commit v3 on v2

--- a/solution.py
+++ b/solution.py
@@ -61,11 +61,11 @@
 
 
 def kernel(
-    grid_hbm, filt, offs, dw_hbm, leg_hbm, sw_hbm, gain_hbm, tab_hbm, tabt_hbm, pf_hbm, pb_hbm, pl_hbm,
-    out_ref,
+    grid_hbm, filt_hbm, offs_hbm, dw_hbm, leg_hbm, sw_hbm, gain_hbm, tab_hbm, tabt_hbm, pf_hbm, pb_hbm, pl_hbm,
+    tiles, disco,
     grid_v, pad, dw, sw, gain, tab, tabt, pf, pb, pleg,
-    legrecv, legp, legn, rows, fsend, frecv, gsend, hrecv, spec, rsend, gback, bsend, ret, ssend, srecv,
-    basis, disco,
+    filt, offs, legrecv, legp, legn, rows, fsend, frecv, gsend, hrecv, spec, rsend, gback, bsend, ret, ssend,
+    basis,
     load_sem, x1_send, x1_recv, leg_send, leg_recv, halo_send, halo_recv,
     a_send, a_recv, b_send, b_recv, c_send, c_recv, d_send, d_recv, e_send, e_recv,
 ):
@@ -107,14 +107,11 @@
         for n, (src, dst) in enumerate(
             (
                 (grid_hbm, grid_v), (tab_hbm, tab), (pf_hbm, pf), (pl_hbm, pleg),
-                (dw_hbm, dw), (sw_hbm, sw), (gain_hbm, gain), (pb_hbm, pb), (tabt_hbm, tabt),
+                (dw_hbm, dw), (sw_hbm, sw), (gain_hbm, gain), (pb_hbm, pb), (tabt_hbm, tabt), (filt_hbm, filt), (offs_hbm, offs),
             )
         )
     ]
-    load_grid, load_tab, load_pf, load_pleg, load_dw, load_sw, load_gain, load_pb, load_tabt = loads
-    for load in loads:
-        load.start()
-
+    load_grid, load_tab, load_pf, load_pleg, load_dw, load_sw, load_gain, load_pb, load_tabt, load_filt, load_offs = loads
     barrier = pltpu.get_barrier_semaphore()
 
     def greet(device):
@@ -180,6 +177,9 @@
         to_rows(
             ch, lambda row: grid_hbm.at[row, :, pl.ds(ch * CW, CW)], rows.at[ch, lon], x1_send.at[ch], x1_recv.at[ch]
         )
+
+    for load in loads:
+        load.start()
 
     load_grid.wait()
     for ct in range(C // 128):
@@ -295,7 +295,8 @@
         ssend[ch] = dot(tabt[...], got).reshape(LON, TILE, CW).astype(bf16)
 
     def send_e(ch):
-        to_tiles(lambda n: ssend.at[ch, n], srecv.at[ch, row_of(lon, ch)], e_send.at[ch], e_recv.at[ch])
+        here = tiles.at[row_of(lon, ch), :, pl.ds(ch * CW, CW)]
+        to_tiles(lambda n: ssend.at[ch, n], here, e_send.at[ch], e_recv)
 
     def with_row(ch, step):
         @pl.when(has_row(lon, ch))
@@ -321,6 +322,8 @@
     with_wavenumber(order_legendre)
 
     load_dw.wait()
+    load_filt.wait()
+    load_offs.wait()
     load_pb.wait()
     load_tabt.wait()
     for copy in halo:
@@ -340,14 +343,7 @@
     for ch in range(CHUNKS):
         with_row(ch, lambda ch: (inverse_fourier(ch), send_e(ch)))
 
-    for ch in range(CHUNKS):
-        cols = slice(ch * CW, (ch + 1) * CW)
-        wait(srecv.at[ch], e_recv.at[ch])
-
-        @pl.loop(0, BAND)
-        def _(i):
-            combined = srecv[ch, i].astype(f32) + disco[pl.ds(i * TILE, TILE), cols]
-            out_ref[i, :, cols] = (grid_v[i, :, cols].astype(f32) + jax.nn.gelu(combined)).astype(bf16)
+    wait(tiles, e_recv)
 
     for copy in halo:
         copy.wait_send()
@@ -390,15 +386,17 @@
 def on_device(grid_field, disco_filter, offsets, disco_weight, legendre, spec_weight, degree_gain):
     bf16 = jnp.bfloat16
     f32 = jnp.float32
-    smem = pl.BlockSpec(memory_space=pltpu.SMEM)
     hbm = pl.BlockSpec(memory_space=pltpu.HBM)
     dma = pltpu.SemaphoreType.DMA
     vmem = pltpu.VMEM
-    return pl.pallas_call(
+    spectral, disco = pl.pallas_call(
         kernel,
-        out_shape=jax.ShapeDtypeStruct(grid_field.shape, bf16),
-        in_specs=[hbm, smem, smem] + [hbm] * 9,
-        out_specs=pl.BlockSpec(memory_space=pltpu.VMEM),
+        out_shape=(
+            vmem(grid_field.shape, bf16),
+            vmem((BAND * TILE, C), f32),
+        ),
+        in_specs=[hbm] * 12,
+        out_specs=(pl.BlockSpec(memory_space=pltpu.VMEM),) * 2,
         scratch_shapes=[
             vmem((BAND, TILE, C), bf16),
             vmem((C // 128, BAND + 4, TILE + 16, 128), f32),
@@ -410,6 +408,8 @@
             vmem((2 * MMAX, 2 * MMAX), bf16),
             vmem((2 * MMAX, 2 * MMAX), bf16),
             vmem((NLAT, NLAT), bf16),
+            pltpu.SMEM((5, KERNELS, BAND), f32),
+            pltpu.SMEM((5, KERNELS, BAND), jnp.int32),
             vmem((LON, LEG, LMAX), bf16),
             vmem((NLAT, LMAX), bf16),
             vmem((LMAX, NLAT), bf16),
@@ -424,10 +424,8 @@
             vmem((CHUNKS, LAT, 2 * MS, CW), bf16),
             vmem((CHUNKS, LAT, 2 * MS, CW), bf16),
             vmem((CHUNKS, LON, TILE, CW), bf16),
-            vmem((CHUNKS, BAND, TILE, CW), bf16),
             vmem((BAND * TILE, KERNELS * C), bf16),
-            vmem((BAND * TILE, C), f32),
-            dma((9,)),
+            dma((11,)),
             dma((CHUNKS,)), dma((CHUNKS,)),
             dma, dma,
             dma((8,)), dma((8,)),
@@ -435,7 +433,7 @@
             dma((CHUNKS,)), dma((CHUNKS,)),
             dma((CHUNKS,)), dma((CHUNKS,)),
             dma((CHUNKS,)), dma((CHUNKS,)),
-            dma((CHUNKS,)), dma((CHUNKS,)),
+            dma((CHUNKS,)), dma,
         ],
         compiler_params=pltpu.CompilerParams(
             collective_id=0, has_side_effects=True, vmem_limit_bytes=62 * 1024 * 1024
@@ -451,6 +449,8 @@
         degree_gain,
         *constant_tables(),
     )
+    combined = spectral.astype(f32) + disco.reshape(grid_field.shape)
+    return (grid_field.astype(f32) + jax.nn.gelu(combined)).astype(bf16)
 
 
 def solution(mesh):

time: 83.9 us -> 81.2 us (0.968)
  Pallas kernels: 81.8 us -> 79.9 us
  local copies, waits for them, and re-layouts: 1.82 us -> 0.01 us
  other arithmetic: 0 us -> 1.17 us
    pallas_call x1, Pallas kernels: 81.8 us -> 79.9 us  [on_device(): pl.pallas_call(kernel, out_shape=(vmem(grid_field.shape, bf16), vmem((BAN...]
    unnamed x1 -> x2, local copies, waits for them, and re-layouts: 1.82 us -> 0.01 us
    convert_element_type x0 -> x1, other arithmetic: none -> 1.17 us  [on_device(): return (grid_field.astype(f32) + jax.nn.gelu(combined)).astype(bf16)]
where the time goes in v3:
time: 81.2 us; the launch traced here: 81.1 us
  Pallas kernels  79.9 us (98%)
  other arithmetic  1.17 us (1%)
    pallas_call x1, Pallas kernels, on_device(): pl.pallas_call(kernel, out_shape=(vmem(grid_field.shape, bf16), vmem((BAN...  79.9 us

profile of v3, /device:TPU:1, one launch (start us, length us, event | category | flops | bytes accessed | tf_op | source)
XLA Modules:
  0.0 81.1 jit_solution(8757971825651221827)
XLA Ops:
  0.0 0.0 copy-start
  0.0 79.9 %shard_map.118 = (bf16[12,48,384]{2,1,0:T(8,128)(2,1)S(1)}, f32[576,384]{1,0:T(8,128)S(1)}) custom-call(bf16[12,48,384]{2,1,0:T(8,128)(2,1)} %grid_hbm.1, f32[5,3,12]{2,1,0:T(4,128)} %bitcast.10, s32[5,3,12]{2,1,0:T(4,128)} %bitcast.11, bf16[1152,384]{1,0:T(8,128)(2,1)} %bitcast.8, bf16[12,24,384]{2,1,0:T(8,128)(2,1)} %bitcast.9, ...), custom_call_target="tpu_custom_call" | custom-call | flops 3000000000 | bytes 8000000 | tf_op jit(solution)/shard_map/pallas_call | solution.py:392
  79.9 0.0 copy-done
  79.9 1.2 %fusion.8 = bf16[12,48,384]{2,1,0:T(8,128)(2,1)} fusion(f32[12,48,384]{2,1,0:T(8,128)S(1)} %bitcast.7, bf16[12,48,384]{2,1,0:T(8,128)(2,1)S(1)} %get-tuple-element.7, bf16[12,48,384]{2,1,0:T(8,128)(2,1)S(1)} %copy-done), kind=kLoop, calls=%fused_computation.9 | loop fusion | flops 2875392 | bytes 2211840 | tf_op jit(solution)/shard_map/convert_element_type | solution.py:453
Async XLA Ops:
  0.0 79.9 %copy-start = (bf16[12,48,384]{2,1,0:T(8,128)(2,1)S(1)}, bf16[12,48,384]{2,1,0:T(8,128)(2,1)}, u32[]{:S(2)}) copy-start(bf16[12,48,384]{2,1,0:T(8,128)(2,1)} %grid_hbm.1) | copy-start | bytes 1327108

commit v4 on v3

--- a/solution.py
+++ b/solution.py
@@ -40,18 +40,12 @@
     values = values.astype(np.float32) * np.float32(1.0 / math.sqrt(NLON))
     table = jnp.asarray(values, jnp.bfloat16)
     table_t = jnp.asarray(values.T.copy(), jnp.bfloat16)
-    perm = np.zeros((2 * MMAX, 2 * MMAX), np.float32)
-    for band in range(LAT):
-        for inner in range(2 * MS):
-            perm[inner * LAT + band, band * 2 * MS + inner] = 1.0
     perm_leg = np.zeros((NLAT, NLAT), np.float32)
     for t in range(NLAT):
         perm_leg[(t % BAND) * LAT + t // BAND, t] = 1.0
     return (
         table,
         table_t,
-        jnp.asarray(perm, jnp.bfloat16),
-        jnp.asarray(perm.T.copy(), jnp.bfloat16),
         jnp.asarray(perm_leg, jnp.bfloat16),
     )
 
@@ -61,9 +55,9 @@
 
 
 def kernel(
-    grid_hbm, filt_hbm, offs_hbm, dw_hbm, leg_hbm, sw_hbm, gain_hbm, tab_hbm, tabt_hbm, pf_hbm, pb_hbm, pl_hbm,
+    grid_hbm, filt_hbm, offs_hbm, dw_hbm, leg_hbm, sw_hbm, gain_hbm, tab_hbm, tabt_hbm, pl_hbm,
     tiles, disco,
-    grid_v, pad, dw, sw, gain, tab, tabt, pf, pb, pleg,
+    grid_v, pad, dw, sw, gain, tab, tabt, pleg,
     filt, offs, legrecv, legp, legn, rows, fsend, frecv, gsend, hrecv, spec, rsend, gback, bsend, ret, ssend,
     basis,
     load_sem, x1_send, x1_recv, leg_send, leg_recv, halo_send, halo_recv,
@@ -106,12 +100,12 @@
         pltpu.make_async_copy(src, dst, load_sem.at[n])
         for n, (src, dst) in enumerate(
             (
-                (grid_hbm, grid_v), (tab_hbm, tab), (pf_hbm, pf), (pl_hbm, pleg),
-                (dw_hbm, dw), (sw_hbm, sw), (gain_hbm, gain), (pb_hbm, pb), (tabt_hbm, tabt), (filt_hbm, filt), (offs_hbm, offs),
+                (grid_hbm, grid_v), (tab_hbm, tab), (pl_hbm, pleg),
+                (dw_hbm, dw), (sw_hbm, sw), (gain_hbm, gain), (tabt_hbm, tabt), (filt_hbm, filt), (offs_hbm, offs),
             )
         )
     ]
-    load_grid, load_tab, load_pf, load_pleg, load_dw, load_sw, load_gain, load_pb, load_tabt, load_filt, load_offs = loads
+    load_grid, load_tab, load_pleg, load_dw, load_sw, load_gain, load_tabt, load_filt, load_offs = loads
     barrier = pltpu.get_barrier_semaphore()
 
     def greet(device):
@@ -231,8 +225,8 @@
 
     def by_wavenumber(ch):
         wait(frecv.at[ch], a_recv.at[ch])
-        got = frecv[ch].astype(f32).reshape(2 * MMAX, CW).astype(bf16)
-        gsend[ch] = dot(pf[...], got).reshape(MS, 2 * LAT, CW).astype(bf16)
+        turned = jnp.swapaxes(frecv[ch].astype(f32), 0, 1)
+        gsend[ch] = turned.reshape(MS, 2 * LAT, CW).astype(bf16)
 
     def send_b(ch):
         to_wavenumbers(lambda m: gsend.at[ch, m], hrecv.at[ch, row_of(lon, ch)], b_send.at[ch], b_recv.at[ch])
@@ -283,8 +277,8 @@
     def by_band(ch):
         wait(gback.at[ch], c_recv.at[ch])
 
-        part = dot(pb[...], gback[ch].reshape(2 * MMAX, CW))
-        bsend[ch] = part.reshape(LAT, 2 * MS, CW).astype(bf16)
+        turned = jnp.swapaxes(gback[ch].astype(f32).reshape(2 * MS, LAT, CW), 0, 1)
+        bsend[ch] = turned.astype(bf16)
 
     def send_d(ch):
         to_bands(lambda q: bsend.at[ch, q], ret.at[ch, lat], d_send.at[ch], d_recv.at[ch])
@@ -312,7 +306,6 @@
     send_legendre()
     for ch in range(CHUNKS):
         with_row(ch, lambda ch: (forward_fourier(ch), send_a(ch)))
-    load_pf.wait()
     for ch in range(CHUNKS):
         with_row(ch, lambda ch: (by_wavenumber(ch), send_b(ch)))
 
@@ -324,7 +317,6 @@
     load_dw.wait()
     load_filt.wait()
     load_offs.wait()
-    load_pb.wait()
     load_tabt.wait()
     for copy in halo:
         copy.wait_recv()
@@ -395,7 +387,7 @@
             vmem(grid_field.shape, bf16),
             vmem((BAND * TILE, C), f32),
         ),
-        in_specs=[hbm] * 12,
+        in_specs=[hbm] * 10,
         out_specs=(pl.BlockSpec(memory_space=pltpu.VMEM),) * 2,
         scratch_shapes=[
             vmem((BAND, TILE, C), bf16),
@@ -405,8 +397,6 @@
             vmem((LMAX, C), f32),
             vmem((2 * MMAX, NLON), bf16),
             vmem((NLON, 2 * MMAX), bf16),
-            vmem((2 * MMAX, 2 * MMAX), bf16),
-            vmem((2 * MMAX, 2 * MMAX), bf16),
             vmem((NLAT, NLAT), bf16),
             pltpu.SMEM((5, KERNELS, BAND), f32),
             pltpu.SMEM((5, KERNELS, BAND), jnp.int32),
@@ -425,7 +415,7 @@
             vmem((CHUNKS, LAT, 2 * MS, CW), bf16),
             vmem((CHUNKS, LON, TILE, CW), bf16),
             vmem((BAND * TILE, KERNELS * C), bf16),
-            dma((11,)),
+            dma((9,)),
             dma((CHUNKS,)), dma((CHUNKS,)),
             dma, dma,
             dma((8,)), dma((8,)),

time: 81.2 us -> 80.2 us (0.988)
  Pallas kernels: 79.9 us -> 78.9 us
    pallas_call x1, Pallas kernels: 79.9 us -> 78.9 us  [on_device(): pl.pallas_call(kernel, out_shape=(vmem(grid_field.shape, bf16), vmem((BAN...]
where the time goes in v4:
time: 80.2 us; the launch traced here: 80.1 us
  Pallas kernels  78.9 us (98%)
  other arithmetic  1.17 us (1%)
    pallas_call x1, Pallas kernels, on_device(): pl.pallas_call(kernel, out_shape=(vmem(grid_field.shape, bf16), vmem((BAN...  78.9 us

profile of v4, /device:TPU:1, one launch (start us, length us, event | category | flops | bytes accessed | tf_op | source)
XLA Modules:
  0.0 80.1 jit_solution(17384294657735105233)
XLA Ops:
  0.0 0.0 copy-start
  0.0 78.9 %shard_map.100 = (bf16[12,48,384]{2,1,0:T(8,128)(2,1)S(1)}, f32[576,384]{1,0:T(8,128)S(1)}) custom-call(bf16[12,48,384]{2,1,0:T(8,128)(2,1)} %grid_hbm.1, f32[5,3,12]{2,1,0:T(4,128)} %bitcast.10, s32[5,3,12]{2,1,0:T(4,128)} %bitcast.11, bf16[1152,384]{1,0:T(8,128)(2,1)} %bitcast.8, bf16[12,24,384]{2,1,0:T(8,128)(2,1)} %bitcast.9, ...), custom_call_target="tpu_custom_call" | custom-call | flops 3000000000 | bytes 8000000 | tf_op jit(solution)/shard_map/pallas_call | solution.py:384
  78.9 0.0 copy-done
  78.9 1.2 %fusion.8 = bf16[12,48,384]{2,1,0:T(8,128)(2,1)} fusion(f32[12,48,384]{2,1,0:T(8,128)S(1)} %bitcast.7, bf16[12,48,384]{2,1,0:T(8,128)(2,1)S(1)} %get-tuple-element.7, bf16[12,48,384]{2,1,0:T(8,128)(2,1)S(1)} %copy-done), kind=kLoop, calls=%fused_computation.9 | loop fusion | flops 2875392 | bytes 2211840 | tf_op jit(solution)/shard_map/convert_element_type | solution.py:443
Async XLA Ops:
  0.0 78.9 %copy-start = (bf16[12,48,384]{2,1,0:T(8,128)(2,1)S(1)}, bf16[12,48,384]{2,1,0:T(8,128)(2,1)}, u32[]{:S(2)}) copy-start(bf16[12,48,384]{2,1,0:T(8,128)(2,1)} %grid_hbm.1) | copy-start | bytes 1327108

commit v5 on v4

--- a/solution.py
+++ b/solution.py
@@ -111,12 +111,9 @@
     def greet(device):
         pl.semaphore_signal(barrier, inc=1, device_id=device, device_id_type=MESH)
 
-    @pl.loop(1, LON)
-    def _(d):
+    for d in range(1, LON):
         greet((lat, lax.rem(lon + d, LON)))
-
-    @pl.loop(1, LAT)
-    def _(d):
+    for d in range(1, LAT):
         greet((lax.rem(lat + d, LAT), lon))
 
     for a in (north, south):
@@ -254,9 +251,12 @@
 
     def legendre(ch):
         wait(hrecv.at[ch], b_recv.at[ch])
+        both = jnp.concatenate(
+            [hrecv[ch, :, r * LAT : (r + 1) * LAT, :].reshape(NLAT, CW) for r in range(2)], axis=1
+        )
+        part = dot(legn[...], both).astype(bf16)
         for r in range(2):
-            part = hrecv[ch, :, r * LAT : (r + 1) * LAT, :].reshape(NLAT, CW)
-            spec[:, r * C + ch * CW : r * C + (ch + 1) * CW] = dot(legn[...], part).astype(bf16)
+            spec[:, r * C + ch * CW : r * C + (ch + 1) * CW] = part[:, r * CW : (r + 1) * CW]
 
     def mix_and_back(ch):
         cols = slice(ch * CW, (ch + 1) * CW)
@@ -266,10 +266,10 @@
             dot(re, sw[0, :, cols]) - dot(im, sw[1, :, cols]),
             dot(re, sw[1, :, cols]) + dot(im, sw[0, :, cols]),
         )
+        values = jnp.concatenate([(part * gain[:, cols]).astype(bf16) for part in filtered], axis=1)
+        back = dot(legp[...], values).astype(bf16)
         for r in range(2):
-            value = (filtered[r] * gain[:, cols]).astype(bf16)
-            back = dot(legp[...], value)
-            rsend[ch, :, r * LAT : (r + 1) * LAT, :] = back.astype(bf16).reshape(BAND, LAT, CW)
+            rsend[ch, :, r * LAT : (r + 1) * LAT, :] = back[:, r * CW : (r + 1) * CW].reshape(BAND, LAT, CW)
 
     def send_c(ch):
         to_rows(ch, lambda row: rsend.at[ch, row], gback.at[ch, my_wavenumber], c_send.at[ch], c_recv.at[ch])

time: 80.2 us -> 80.5 us (level)
  no operation moved by 1% of the time
where the time goes in v5:
time: 80.5 us; the launch traced here: 80.4 us
  Pallas kernels  79.2 us (98%)
  other arithmetic  1.17 us (1%)
    pallas_call x1, Pallas kernels, on_device(): pl.pallas_call(kernel, out_shape=(vmem(grid_field.shape, bf16), vmem((BAN...  79.2 us

profile of v5, /device:TPU:1, one launch (start us, length us, event | category | flops | bytes accessed | tf_op | source)
XLA Modules:
  0.0 80.4 jit_solution(3115574003537882761)
XLA Ops:
  0.0 0.0 copy-start
  0.0 79.2 %shard_map.100 = (bf16[12,48,384]{2,1,0:T(8,128)(2,1)S(1)}, f32[576,384]{1,0:T(8,128)S(1)}) custom-call(bf16[12,48,384]{2,1,0:T(8,128)(2,1)} %grid_hbm.1, f32[5,3,12]{2,1,0:T(4,128)} %bitcast.10, s32[5,3,12]{2,1,0:T(4,128)} %bitcast.11, bf16[1152,384]{1,0:T(8,128)(2,1)} %bitcast.8, bf16[12,24,384]{2,1,0:T(8,128)(2,1)} %bitcast.9, ...), custom_call_target="tpu_custom_call" | custom-call | flops 3000000000 | bytes 8000000 | tf_op jit(solution)/shard_map/pallas_call | solution.py:384
  79.2 0.0 copy-done
  79.2 1.2 %fusion.8 = bf16[12,48,384]{2,1,0:T(8,128)(2,1)} fusion(f32[12,48,384]{2,1,0:T(8,128)S(1)} %bitcast.7, bf16[12,48,384]{2,1,0:T(8,128)(2,1)S(1)} %get-tuple-element.7, bf16[12,48,384]{2,1,0:T(8,128)(2,1)S(1)} %copy-done), kind=kLoop, calls=%fused_computation.9 | loop fusion | flops 2875392 | bytes 2211840 | tf_op jit(solution)/shard_map/convert_element_type | solution.py:443
Async XLA Ops:
  0.0 79.2 %copy-start = (bf16[12,48,384]{2,1,0:T(8,128)(2,1)S(1)}, bf16[12,48,384]{2,1,0:T(8,128)(2,1)}, u32[]{:S(2)}) copy-start(bf16[12,48,384]{2,1,0:T(8,128)(2,1)} %grid_hbm.1) | copy-start | bytes 1327108
